TPU v7x, 512 devices: a whole 4x8x8 slice. The times are simulated.
512 devices in a mesh: wide: 64 (over z, x, core), narrow: 8 (over y).
Axes of the slice: x: 4, y: 8, z: 8, core: 2. Of those that a mesh axis runs over, the one named last changes fastest.
Arguments:
- source: float32 [512, 256, 256], P('wide', 'narrow'), may hold values from -24 to 24
- face_x: float32 [512, 256, 256], P('wide', 'narrow'), may hold values from 0.25 to 4
- face_y: float32 [512, 256, 256], P('wide', 'narrow'), may hold values from 0.25 to 4
- face_z: float32 [512, 256, 256], P('wide', 'narrow'), may hold values from 0.25 to 4
Outputs:
- pressure: float32 [512, 256, 256], P('wide', 'narrow')
- residual: float32 [512, 256, 256], P('wide', 'narrow')
All inputs are finite; a program needn't handle non-finite values.
Results may differ from a plain program's by a relative error of at most 0.00035.
Values sent between devices are 32-bit elements; how exact they have to be, the bound alone decides.
A program may use at most 128 MiB of HBM per device.

v0:
```python
import jax
import jax.numpy as jnp
from jax import lax
from jax.sharding import PartitionSpec as P

CGI = 6


relax = 0.8
depth = 3


def padded_2(cells, sides, width):
    for axis, dim in sides:
        count = lax.axis_size(axis)
        ends = count - 1
        head = lax.slice_in_dim(cells, 0, width, axis=dim)
        tail = lax.slice_in_dim(cells, cells.shape[dim] - width, cells.shape[dim], axis=dim)
        cells = jnp.concatenate(
            [
                lax.ppermute(tail, axis, [(i, (i + 1) % count) for i in range(ends)]),
                cells,
                lax.ppermute(head, axis, [((i + 1) % count, i) for i in range(ends)]),
            ],
            axis=dim,
        )
    return cells


def passed_along(value, axis, steps):
    count = lax.axis_size(axis)
    leading, last = (max(0, -steps), min(count, count - steps))
    return lax.ppermute(value, axis, [(source, source + steps) for source in range(leading, last)])


def pair_sum(array, which):
    shape = array.shape
    folded = shape[:which] + (shape[which] // 2, 2) + shape[which + 1 :]
    return jnp.sum(array.reshape(folded), axis=which + 1)


def restrict(remain):
    return pair_sum(pair_sum(pair_sum(remain, 0), 1), 2)


def prolong(coarse):
    return jnp.repeat(jnp.repeat(jnp.repeat(coarse, 2, axis=0), 2, axis=1), 2, axis=2)


def coarsen(faces):
    face_x, face_y, face_z, plane_x, plane_y = faces
    return (
        pair_sum(pair_sum(face_x[1::2], 1), 2),
        pair_sum(pair_sum(face_y[:, 1::2], 0), 2),
        pair_sum(pair_sum(face_z[:, :, 1::2], 0), 1),
        pair_sum(pair_sum(plane_x, 1), 2),
        pair_sum(pair_sum(plane_y, 0), 2),
    )


def complete(faces):
    face_x, face_y, face_z, plane_x, plane_y = faces
    low_x = jnp.concatenate([plane_x, face_x[:-1]], axis=0)
    low_y = jnp.concatenate([plane_y, face_y[:, :-1]], axis=1)
    low_z = jnp.concatenate([jnp.zeros_like(face_z[:, :, :1]), face_z[:, :, :-1]], axis=2)
    diagonal = face_x + low_x + face_y + low_y + face_z + low_z
    return (face_x, face_y, face_z, low_x, low_y, low_z, diagonal)


def surround(field, layout):
    if layout == "both":
        padded = padded_2(field, (("wide", 0), ("narrow", 1)), 1)
        return jnp.pad(padded, ((0, 0), (0, 0), (1, 1)))
    padded = padded_2(field, (("wide", 0),), 1)
    return jnp.pad(padded, ((0, 0), (1, 1), (1, 1)))


def operate(field, coeffs, layout):
    face_x, face_y, face_z, low_x, low_y, low_z, diagonal = coeffs
    padded = surround(field, layout)
    beside_all = face_x * padded[2:, 1:-1, 1:-1] + low_x * padded[:-2, 1:-1, 1:-1]
    beside_all = beside_all + face_y * padded[1:-1, 2:, 1:-1] + low_y * padded[1:-1, :-2, 1:-1]
    beside_all = beside_all + face_z * padded[1:-1, 1:-1, 2:] + low_z * padded[1:-1, 1:-1, :-2]
    return diagonal * field - beside_all


def global_dot(value):
    return lax.psum(value, "wide")


def conjugate(source, coeffs, layout):
    solved = jnp.zeros_like(source)
    remain = source
    direction = source
    norm_now = jnp.sum(remain * remain)
    norm_now = global_dot(norm_now)
    for counter in range(CGI):
        image = operate(direction, coeffs, layout)
        curvature = jnp.sum(direction * image)
        curvature = global_dot(curvature)
        alpha = norm_now / curvature
        solved = solved + alpha * direction
        remain = remain - alpha * image
        norm_next = jnp.sum(remain * remain)
        norm_next = global_dot(norm_next)
        direction = remain + norm_next / norm_now * direction
        norm_now = norm_next
    return solved


def coarse_solve(source, faces):
    return conjugate(source, complete(faces), "wide")


def cycle(level, source, faces, merged, merge_at):
    coeffs = complete(faces)
    layout = "wide" if merged else "both"
    diagonal = coeffs[6]
    field = relax * source / diagonal
    field = field + relax * (source - operate(field, coeffs, layout)) / diagonal
    remain = source - operate(field, coeffs, layout)
    coarse_source = restrict(remain)
    coarse_faces = coarsen(faces)
    joined = not merged and level + 1 == merge_at
    kept = coarse_source.shape[1]
    if joined:
        coarse_source, gath_x, gath_y, gath_z, gath_plane = (
            lax.all_gather(coarse_source, "narrow", axis=1, tiled=True),
            lax.all_gather(coarse_faces[0], "narrow", axis=1, tiled=True),
            lax.all_gather(coarse_faces[1], "narrow", axis=1, tiled=True),
            lax.all_gather(coarse_faces[2], "narrow", axis=1, tiled=True),
            lax.all_gather(coarse_faces[3], "narrow", axis=1, tiled=True),
        )
        coarse_faces = (gath_x, gath_y, gath_z, gath_plane, jnp.zeros_like(gath_y[:, :1]))
    if level + 1 == depth:
        correction = coarse_solve(coarse_source, coarse_faces)
    else:
        correction = cycle(level + 1, coarse_source, coarse_faces, merged or joined, merge_at)[0]
    if joined:
        correction = lax.dynamic_slice_in_dim(correction, lax.axis_index("narrow") * kept, kept, 1)
    field = field + prolong(correction)
    for sweeping in range(2):
        field = field + relax * (source - operate(field, coeffs, layout)) / diagonal
    return (field, coeffs)


def shards(source, face_x, face_y, face_z):
    plane_x = passed_along(face_x[-1:], "wide", 1)
    plane_y = passed_along(face_y[:, -1:], "narrow", 1)
    merge_at = 2
    pressure, coeffs = cycle(0, source, (face_x, face_y, face_z, plane_x, plane_y), False, merge_at)
    residual = source - operate(pressure, coeffs, "both")
    return (pressure, residual)


def solution(mesh):
    return jax.shard_map(
        shards,
        mesh=mesh,
        in_specs=(
            P("wide", "narrow", None),
            P("wide", "narrow", None),
            P("wide", "narrow", None),
            P("wide", "narrow", None),
        ),
        out_specs=(P("wide", "narrow", None), P("wide", "narrow", None)),
        check_vma=False,
    )
```

profile of v0, /device:TPU:199, one launch (start us, length us, event | category | flops | bytes accessed | tf_op | source)
XLA Modules:
  0.0 1849.6 jit_solution(8814541994053725824)
XLA Ops:
  1.5 5.7 collective-permute-start
  13.8 19.2 %all_gather.16 = f32[2,64,64]{2,0,1:T(2,128)S(1)} all-gather(f32[2,8,64]{2,0,1:T(2,128)S(1)} %copy.1447), channel_id=1, replica_groups=mesh['wide'=64,'narrow'=8] {'narrow'}, dimensions={1}, use_global_device_ids=true | all-gather | bytes 36864 | tf_op jit(solution)/shard_map/all_gather | solution.py:129
  33.2 8.3 collective-permute-start.3
  43.6 6.4 collective-permute-done.2
  50.1 3.6 collective-permute-start.5
  64.2 4.5 slice.664
  80.2 6.0 collective-permute-start.11
  88.5 6.1 collective-permute-done.10
  99.5 19.7 %all_gather.18 = f32[2,64,64]{2,0,1:T(2,128)S(1)} all-gather(f32[2,8,64]{2,0,1:T(2,128)S(1)} %copy.1453), channel_id=1, replica_groups=mesh['wide'=64,'narrow'=8] {'narrow'}, dimensions={1}, use_global_device_ids=true | all-gather | bytes 36864 | tf_op jit(solution)/shard_map/all_gather | solution.py:130
  119.6 8.4 collective-permute-start.15
  129.9 18.4 all_gather.19
  153.1 19.4 %all-gather = f32[64,64]{1,0:T(8,128)S(1)} all-gather(f32[8,64]{1,0:T(8,128)S(1)} %copy.1450), channel_id=2, replica_groups=mesh['wide'=64,'narrow'=8] {'narrow'}, dimensions={0}, use_global_device_ids=true | all-gather | bytes 18432 | tf_op jit(solution)/shard_map/all_gather | solution.py:132
  173.1 18.3 all_gather.15
  191.7 26.5 %collective-permute-start.19 = (f32[1,64,64]{2,0,1:T(1,128)S(1)}, f32[1,64,64]{2,0,1:T(1,128)S(1)}, u32[]{:S(2)}, u32[]{:S(2)}) collective-permute-start(f32[1,64,64]{2,0,1:T(1,128)S(1)} %get-tuple-element.72), channel_id=1, source_target_pairs={{0,8},{8,16},{16,24},{24,32},{32,40},{40,48},{48,56},{56,64},{64,7... | collective-permute-start | bytes 49160 | tf_op jit(solution)/shard_map/ppermute | solution.py:21
  220.3 6.4 collective-permute-done.18
  233.9 4.0 collective-permute-done.20
  243.9 5.8 collective-permute-done.22
  250.6 124.1 %all-reduce.25 = (f32[]{:T(128)}, f32[]{:T(128)}) all-reduce(f32[]{:T(128)} %multiply_reduce_fusion.10, f32[]{:T(128)} %get-tuple-element.38), channel_id=1, replica_groups=mesh['wide'=64,'narrow'=8] {'wide'}, use_global_device_ids=true, to_apply=%region_28.29 | all-reduce | flops 2 | bytes 16 | tf_op jit(solution)/shard_map/psum | solution.py:88
  376.6 124.7 %psum.86 = f32[]{:T(128)} all-reduce(f32[]{:T(128)} %multiply_reduce_fusion.8), channel_id=1, replica_groups=mesh['wide'=64,'narrow'=8] {'wide'}, use_global_device_ids=true, to_apply=%region_40.41 | all-reduce | flops 1 | bytes 8 | tf_op jit(solution)/shard_map/psum | solution.py:88
  502.7 7.5 collective-permute-start.25
  512.1 6.4 collective-permute-done.24
  519.3 124.1 %psum.87 = f32[]{:T(128)} all-reduce(f32[]{:T(128)} %get-tuple-element.36), channel_id=1, replica_groups=mesh['wide'=64,'narrow'=8] {'wide'}, use_global_device_ids=true, to_apply=%region_42.43 | all-reduce | flops 1 | bytes 8 | tf_op jit(solution)/shard_map/psum | solution.py:88
  645.4 124.7 %psum.88 = f32[]{:T(128)} all-reduce(f32[]{:T(128)} %get-tuple-element.34), channel_id=1, replica_groups=mesh['wide'=64,'narrow'=8] {'wide'}, use_global_device_ids=true, to_apply=%region_44.45 | all-reduce | flops 1 | bytes 8 | tf_op jit(solution)/shard_map/psum | solution.py:88
  771.4 7.5 collective-permute-start.27
  780.9 6.4 collective-permute-done.26
  788.1 124.1 %psum.89 = f32[]{:T(128)} all-reduce(f32[]{:T(128)} %get-tuple-element.32), channel_id=1, replica_groups=mesh['wide'=64,'narrow'=8] {'wide'}, use_global_device_ids=true, to_apply=%region_46.47 | all-reduce | flops 1 | bytes 8 | tf_op jit(solution)/shard_map/psum | solution.py:88
  914.2 124.7 %psum.90 = f32[]{:T(128)} all-reduce(f32[]{:T(128)} %get-tuple-element.30), channel_id=1, replica_groups=mesh['wide'=64,'narrow'=8] {'wide'}, use_global_device_ids=true, to_apply=%region_48.49 | all-reduce | flops 1 | bytes 8 | tf_op jit(solution)/shard_map/psum | solution.py:88
  1040.2 7.5 collective-permute-start.29
  1049.7 6.4 collective-permute-done.28
  1056.9 124.1 %psum.91 = f32[]{:T(128)} all-reduce(f32[]{:T(128)} %get-tuple-element.28), channel_id=1, replica_groups=mesh['wide'=64,'narrow'=8] {'wide'}, use_global_device_ids=true, to_apply=%region_50.51 | all-reduce | flops 1 | bytes 8 | tf_op jit(solution)/shard_map/psum | solution.py:88
  1183.0 124.7 %psum.92 = f32[]{:T(128)} all-reduce(f32[]{:T(128)} %get-tuple-element.26), channel_id=1, replica_groups=mesh['wide'=64,'narrow'=8] {'wide'}, use_global_device_ids=true, to_apply=%region_52.53 | all-reduce | flops 1 | bytes 8 | tf_op jit(solution)/shard_map/psum | solution.py:88
  1309.0 7.5 collective-permute-start.31
  1318.5 6.4 collective-permute-done.30
  1325.7 124.1 %psum.93 = f32[]{:T(128)} all-reduce(f32[]{:T(128)} %get-tuple-element.24), channel_id=1, replica_groups=mesh['wide'=64,'narrow'=8] {'wide'}, use_global_device_ids=true, to_apply=%region_54.55 | all-reduce | flops 1 | bytes 8 | tf_op jit(solution)/shard_map/psum | solution.py:88
  1451.8 124.7 %psum.94 = f32[]{:T(128)} all-reduce(f32[]{:T(128)} %multiply_reduce_fusion), channel_id=1, replica_groups=mesh['wide'=64,'narrow'=8] {'wide'}, use_global_device_ids=true, to_apply=%region_56.57 | all-reduce | flops 1 | bytes 8 | tf_op jit(solution)/shard_map/psum | solution.py:88
  1577.8 7.5 collective-permute-start.33
  1587.2 6.4 collective-permute-done.32
  1594.5 124.1 %psum.95 = f32[]{:T(128)} all-reduce(f32[]{:T(128)} %fusion.164), channel_id=1, replica_groups=mesh['wide'=64,'narrow'=8] {'wide'}, use_global_device_ids=true, to_apply=%region_58.59 | all-reduce | flops 1 | bytes 8 | tf_op jit(solution)/shard_map/psum | solution.py:88
  1720.3 7.5 collective-permute-start.35
  1729.8 6.6 collective-permute-done.34
  1741.5 6.1 collective-permute-done.36
  1753.1 5.9 collective-permute-done.38
  1762.5 3.9 collective-permute-done.40
  1771.7 6.4 collective-permute-done.42
  1792.4 6.6 collective-permute-done.46
  1799.1 4.1 collective-permute-start.49
  1813.6 6.6 collective-permute-done.50
  1834.3 6.6 collective-permute-done.54
  (264 shorter events, 147.7 us)
Async XLA Ops:
  1.5 31.5 %collective-permute-start = (f32[1,32,256]{2,1,0:T(8,128)S(1)}, f32[1,32,256]{2,1,0:T(8,128)S(1)}, u32[]{:S(2)}, u32[]{:S(2)}) collective-permute-start(f32[1,32,256]{2,1,0:T(8,128)S(1)} %slice.635), channel_id=1, source_target_pairs={{0,8},{8,16},{16,24},{24,32},{32,40},{40,48},{48,56},{56,64},{64,7... | collective-permute-start | bytes 98312 | tf_op jit(solution)/shard_map/ppermute | solution.py:33
  8.0 24.9 %collective-permute-start.1 = (f32[8,1,256]{2,0,1:T(8,128)S(1)}, f32[8,1,256]{2,0,1:T(8,128)S(1)}, u32[]{:S(2)}, u32[]{:S(2)}) collective-permute-start(f32[8,1,256]{2,0,1:T(8,128)S(1)} %copy.1493), channel_id=1, source_target_pairs={{0,1},{1,2},{2,3},{3,4},{4,5},{5,6},{6,7},{8,9},{9,10},{10,11},{11... | collective-permute-start | bytes 24584 | tf_op jit(solution)/shard_map/ppermute | solution.py:33
  33.2 10.4 collective-permute-start.3
  41.5 8.6 collective-permute-start.2
  50.1 6.6 collective-permute-start.5
  58.9 9.8 collective-permute-start.7
  62.2 8.6 collective-permute-start.6
  70.8 5.9 collective-permute-start.9
  80.2 8.2 collective-permute-start.11
  86.3 8.3 collective-permute-start.10
  94.6 24.7 %collective-permute-start.13 = (f32[6,1,128]{2,1,0:T(1,128)S(1)}, f32[6,1,128]{2,1,0:T(1,128)S(1)}, u32[]{:S(2)}, u32[]{:S(2)}) collective-permute-start(f32[6,1,128]{2,1,0:T(1,128)S(1)} %get-tuple-element.80), channel_id=1, source_target_pairs={{0,1},{1,2},{2,3},{3,4},{4,5},{5,6},{6,7},{8,9},{9,10},{10,11},{11... | collective-permute-start | bytes 9224 | tf_op jit(solution)/shard_map/ppermute | solution.py:21
  98.2 21.1 %collective-permute-start.12 = (f32[6,1,128]{2,1,0:T(1,128)S(1)}, f32[6,1,128]{2,1,0:T(1,128)S(1)}, u32[]{:S(2)}, u32[]{:S(2)}) collective-permute-start(f32[6,1,128]{2,1,0:T(1,128)S(1)} %get-tuple-element.81), channel_id=1, source_target_pairs={{1,0},{2,1},{3,2},{4,3},{5,4},{6,5},{7,6},{9,8},{10,9},{11,10},{12... | collective-permute-start | bytes 9224 | tf_op jit(solution)/shard_map/ppermute | solution.py:23
  119.6 29.0 %collective-permute-start.15 = (f32[1,16,128]{2,1,0:T(8,128)S(1)}, f32[1,16,128]{2,1,0:T(8,128)S(1)}, u32[]{:S(2)}, u32[]{:S(2)}) collective-permute-start(f32[1,16,128]{2,1,0:T(8,128)S(1)} %get-tuple-element.86), channel_id=1, source_target_pairs={{0,8},{8,16},{16,24},{24,32},{32,40},{40,48},{48,56},{56,64},{64,7... | collective-permute-start | bytes 24584 | tf_op jit(solution)/shard_map/ppermute | solution.py:21
  127.9 20.6 %collective-permute-start.14 = (f32[1,16,128]{2,1,0:T(8,128)S(1)}, f32[1,16,128]{2,1,0:T(8,128)S(1)}, u32[]{:S(2)}, u32[]{:S(2)}) collective-permute-start(f32[1,16,128]{2,1,0:T(8,128)S(1)} %get-tuple-element.87), channel_id=1, source_target_pairs={{8,0},{16,8},{24,16},{32,24},{40,32},{48,40},{56,48},{64,56},{72,6... | collective-permute-start | bytes 24584 | tf_op jit(solution)/shard_map/ppermute | solution.py:23
  148.6 23.9 %collective-permute-start.17 = (f32[6,1,128]{2,1,0:T(1,128)S(1)}, f32[6,1,128]{2,1,0:T(1,128)S(1)}, u32[]{:S(2)}, u32[]{:S(2)}) collective-permute-start(f32[6,1,128]{2,1,0:T(1,128)S(1)} %get-tuple-element.78), channel_id=1, source_target_pairs={{0,1},{1,2},{2,3},{3,4},{4,5},{5,6},{6,7},{8,9},{9,10},{10,11},{11... | collective-permute-start | bytes 9224 | tf_op jit(solution)/shard_map/ppermute | solution.py:21
  151.8 20.7 %collective-permute-start.16 = (f32[6,1,128]{2,1,0:T(1,128)S(1)}, f32[6,1,128]{2,1,0:T(1,128)S(1)}, u32[]{:S(2)}, u32[]{:S(2)}) collective-permute-start(f32[6,1,128]{2,1,0:T(1,128)S(1)} %get-tuple-element.79), channel_id=1, source_target_pairs={{1,0},{2,1},{3,2},{4,3},{5,4},{6,5},{7,6},{9,8},{10,9},{11,10},{12... | collective-permute-start | bytes 9224 | tf_op jit(solution)/shard_map/ppermute | solution.py:23
  191.7 28.6 %collective-permute-start.19 = (f32[1,64,64]{2,0,1:T(1,128)S(1)}, f32[1,64,64]{2,0,1:T(1,128)S(1)}, u32[]{:S(2)}, u32[]{:S(2)}) collective-permute-start(f32[1,64,64]{2,0,1:T(1,128)S(1)} %get-tuple-element.72), channel_id=1, source_target_pairs={{0,8},{8,16},{16,24},{24,32},{32,40},{40,48},{48,56},{56,64},{64,7... | collective-permute-start | bytes 49160 | tf_op jit(solution)/shard_map/ppermute | solution.py:21
  218.2 8.6 collective-permute-start.18
  227.5 6.4 collective-permute-start.21
  229.4 8.6 collective-permute-start.20
  238.9 5.0 collective-permute-start.23
  241.4 8.4 collective-permute-start.22
  502.7 9.4 collective-permute-start.25
  510.2 8.4 collective-permute-start.24
  771.4 9.4 collective-permute-start.27
  779.0 8.4 collective-permute-start.26
  1040.2 9.4 collective-permute-start.29
  1047.7 8.4 collective-permute-start.28
  1309.0 9.4 collective-permute-start.31
  1316.5 8.4 collective-permute-start.30
  1577.8 9.4 collective-permute-start.33
  1585.3 8.4 collective-permute-start.32
  1720.3 9.4 collective-permute-start.35
  1727.8 8.6 collective-permute-start.34
  1739.1 8.6 collective-permute-start.36
  1750.6 8.3 collective-permute-start.38
  1761.2 5.2 collective-permute-start.40
  1766.7 5.0 collective-permute-start.43
  1769.8 8.3 collective-permute-start.42
  1778.1 4.9 collective-permute-start.45
  1787.1 5.3 collective-permute-start.47
  1790.5 8.6 collective-permute-start.46
  1799.1 5.4 collective-permute-start.49
  1808.6 5.0 collective-permute-start.51
  1811.7 8.6 collective-permute-start.50
  1820.2 4.9 collective-permute-start.53
  1829.1 5.3 collective-permute-start.55
  1832.4 8.6 collective-permute-start.54
  (15 other events, 133.4 us)
where the time goes:
time: 1850 us
  blocking collectives  1460 us (79%)
  starting transfers between devices  207 us (11%)
  waiting for transfers between devices  128 us (7%)
  other arithmetic  20.9 us (1%)
    psum x11, blocking collectives, global_dot(): return lax.psum(value, 'wide')  1370 us
    ppermute x28, starting transfers between devices, padded_2(): lax.ppermute(tail, axis, [(i, (i + 1) % count) for i in range(ends)])  148 us
    ppermute x28, waiting for transfers between devices, padded_2(): lax.ppermute(head, axis, [((i + 1) % count, i) for i in range(ends)])  128 us
    ppermute x28, starting transfers between devices, padded_2(): lax.ppermute(head, axis, [((i + 1) % count, i) for i in range(ends)])  49.8 us
  transfers between devices with their start and end apart: 58, of which 25 were waited for; matrix products, arithmetic and copies ran while one was open for 1% of the time, Pallas kernels for 0%

commit v1 on v0

v1 whole, which is shorter than its diff:
```python
import functools

import jax
import jax.numpy as jnp
from jax import lax
from jax.experimental import pallas as pl
from jax.experimental.pallas import tpu as pltpu
from jax.sharding import PartitionSpec as P

CGI = 6
relax = 0.8
MESH = pl.DeviceIdType.MESH
F32 = jnp.float32
BF16 = jnp.bfloat16


def iota(shape, dim):
    return lax.broadcasted_iota(jnp.int32, shape, dim)


def picked(values, chosen):
    high = values.astype(BF16)
    rest = values - high.astype(F32)
    middle = rest.astype(BF16)
    low = (rest - middle.astype(F32)).astype(BF16)
    product = functools.partial(jnp.dot, preferred_element_type=F32)
    return product(high, chosen) + product(middle, chosen) + product(low, chosen)


def ones_where(condition):
    return jnp.where(condition, 1.0, 0.0).astype(BF16)


def next_z(cells):
    lanes = cells.shape[-1]
    lane = iota(cells.shape[:-1] + (128,), len(cells.shape) - 1)
    axis = len(cells.shape) - 1
    if lanes == 128:
        return jnp.where(lane == 127, 0.0, pltpu.roll(cells, 127, axis))
    first = pltpu.roll(cells[..., :128], 127, axis)
    second = pltpu.roll(cells[..., 128:], 127, axis)
    return jnp.concatenate([jnp.where(lane == 127, second, first), jnp.where(lane == 127, 0.0, second)], axis=axis)


def last_z(cells):
    lanes = cells.shape[-1]
    lane = iota(cells.shape[:-1] + (128,), len(cells.shape) - 1)
    axis = len(cells.shape) - 1
    if lanes == 128:
        return jnp.where(lane == 0, 0.0, pltpu.roll(cells, 1, axis))
    first = pltpu.roll(cells[..., :128], 1, axis)
    second = pltpu.roll(cells[..., 128:], 1, axis)
    return jnp.concatenate([jnp.where(lane == 0, 0.0, first), jnp.where(lane == 0, first, second)], axis=axis)


def remainder(b, f, v, p):
    here = v[p]
    rows = here.shape[0]
    flow = f[0, p] * (v[p + 1] - here) - f[0, p - 1] * (here - v[p - 1])
    along = f[1, p] * (pltpu.roll(here, rows - 1, 0) - here)
    flow = flow + (along - pltpu.roll(along, 1, 0))
    along = f[2, p] * (next_z(here) - here)
    flow = flow + (along - last_z(along))
    return b[p] + flow


def diagonal(f, p):
    return (f[0, p] + f[0, p - 1]) + (f[1, p] + pltpu.roll(f[1, p], 1, 0)) + (f[2, p] + last_z(f[2, p]))


def body(sizes, src, inx, iny, inz, out_p, out_r, IN, PKs, FYs, FYr, RK, W0, VA, VD, VB, VY, VE, VF, RZ, U0,
         F1, F1S, B1, B1S, W1, X1, Y1, Y1R, Y1S, Z1, U1, F2, F2S, B2, B2S, W2, X2, Y2, Y2R, Y2S, Z2,
         T3s, T3r, G3f, B3s, B3r, G3b, EG, YG, ZG, PD, RR, QQ, XS, send_sem, recv_sem, load_sem, store_sem):
    wide, narrow, ring, group = sizes
    i, j = lax.axis_index("wide"), lax.axis_index("narrow")
    zi, ri = lax.div(i, group), lax.rem(i, group)

    def wide_at(step):
        return lax.rem(i + (step + wide), wide)

    def narrow_at(step):
        return lax.rem(j + (step + narrow), narrow)

    loads = []
    for number, ref in enumerate((inx, iny, inz, src)):
        loads.append(pltpu.make_async_copy(ref, IN.at[number, pl.ds(3, 8), pl.ds(0, 32)], load_sem.at[number]))
        loads[-1].start()

    barrier = pltpu.get_barrier_semaphore()
    partners = [(wide_at(a), narrow_at(b)) for a in range(-2, 3) for b in range(-1, 2) if (a, b) != (0, 0)]
    partners += [(i, narrow_at(d)) for d in range(2, narrow - 1)]
    partners += [(lax.rem(zi + d, ring) * group + ri, j) for d in range(1, ring)]
    partners += [(zi * group + lax.rem(ri + d, group), j) for d in range(1, group)]
    for partner in partners:
        pl.semaphore_signal(barrier, inc=1, device_id=partner, device_id_type=MESH)

    sent = []

    def send(source, target, partner):
        number = len(sent)
        copy = pltpu.make_async_remote_copy(
            src_ref=source, dst_ref=target, send_sem=send_sem.at[number], recv_sem=recv_sem.at[number],
            device_id=partner, device_id_type=MESH)
        copy.start()
        sent.append(copy)
        return copy

    def arrive(copies):
        for copy in copies:
            copy.wait_recv()

    def exchange(source, target, stage, own, rows, far):
        near, later = [], []
        for a in sorted(range(-far, far + 1), key=abs):
            for b in (0, 1, -1):
                if (a, b) == (0, 0):
                    continue
                start = 4 - a * own
                low, high = max(start, 0), min(start + own, 8 + own)
                from_low = 4 + low - start
                partner = (wide_at(-a), narrow_at(-b))
                if b == 0:
                    piece = source.at[:, pl.ds(4, own), pl.ds(0, rows)]
                    place = target.at[:, pl.ds(4 + a * own, own), pl.ds(0, rows)]
                else:
                    piece = source.at[:, pl.ds(4, own), pl.ds(rows - 8 if b == -1 else 0, 8)]
                    place = stage.at[0 if b == -1 else 1, :, pl.ds(4 + a * own, own)]
                copy = send(piece, place, partner)
                (near if abs(a) < 2 else later).append(copy)
        return near, later

    tile_row = iota((8, 128), 0)
    row256 = iota((8, 256), 0)

    def merged(stage, field, plane):
        return jnp.where(tile_row < 4, stage[1, field, plane], stage[0, field, plane])

    for copy in loads:
        copy.wait()

    @pl.loop(0, 8)
    def pack(p):
        up = jnp.zeros((8, 256), F32)
        down = jnp.zeros((8, 256), F32)
        for f in range(4):
            mine = (row256 >> 1) == f
            up = jnp.where(mine, pltpu.roll(IN[f, 3 + p, 24:32], (2 * f + 2) % 8, 0), up)
            down = jnp.where(mine, pltpu.roll(IN[f, 3 + p, 0:8], 2 * f, 0), down)
        PKs[0, p] = up
        PKs[1, p] = down

    for p in range(8):
        FYs[p:p + 1] = IN[1, 3 + p, 29:30]

    pl.semaphore_wait(barrier, len(partners))

    first = []
    first.append(send(IN.at[:, pl.ds(9, 2), pl.ds(0, 32)], IN.at[:, pl.ds(1, 2), pl.ds(0, 32)], (wide_at(1), j)))
    first.append(send(IN.at[:, pl.ds(3, 2), pl.ds(0, 32)], IN.at[:, pl.ds(11, 2), pl.ds(0, 32)], (wide_at(-1), j)))
    first.append(send(IN.at[0, pl.ds(8, 1), pl.ds(0, 32)], IN.at[0, pl.ds(0, 1), pl.ds(0, 32)], (wide_at(1), j)))
    for side, b in ((0, 1), (1, -1)):
        first.append(send(PKs.at[side], RK.at[side, pl.ds(2, 8)], (i, narrow_at(b))))
        first.append(send(PKs.at[side, pl.ds(6, 2)], RK.at[side, pl.ds(0, 2)], (wide_at(1), narrow_at(b))))
        first.append(send(PKs.at[side, pl.ds(0, 2)], RK.at[side, pl.ds(10, 2)], (wide_at(-1), narrow_at(b))))
    first.append(send(FYs, FYr, (i, narrow_at(1))))

    pairs0 = ones_where((iota((256, 128), 0) >> 1) == iota((256, 128), 1))
    odds0 = ones_where(iota((256, 128), 0) == 2 * iota((256, 128), 1) + 1)
    pairs1 = ones_where((iota((128, 128), 0) >> 1) == iota((128, 128), 1))
    odds1 = ones_where(iota((128, 128), 0) == 2 * iota((128, 128), 1) + 1)
    pairs2 = ones_where((iota((128, 128), 0) >> 1) == (iota((128, 128), 1) & 31))
    odds2 = ones_where(iota((128, 128), 0) == 2 * (iota((128, 128), 1) & 31) + 1)

    def paired(tiles, odd_only=False):
        lanes = tiles[0].shape[1]
        half = tiles[0].shape[0] // 2
        for c, tile in enumerate(tiles):
            for part in range(lanes // 128):
                RZ[part, c, 0:2 * half] = tile[:, 128 * part:128 * (part + 1)]
        below = []
        for c in range(len(tiles)):
            beside = []
            for part in range(lanes // 128):
                odd = RZ[part, c, pl.ds(1, half, stride=2), :]
                beside.append(odd if odd_only else RZ[part, c, pl.ds(0, half, stride=2), :] + odd)
            below.append(jnp.concatenate(beside, axis=1) if len(beside) > 1 else beside[0])
        return jnp.concatenate(below, axis=0)

    def coarse_faces(f, at, target, own, rows, pairs, odds):
        half = rows // 2
        x = [f[0, at + 2 * c + 1, 0:rows] for c in range(own)]
        y = [f[1, at + 2 * c, 0:rows] + f[1, at + 2 * c + 1, 0:rows] for c in range(own)]
        z = [f[2, at + 2 * c, 0:rows] + f[2, at + 2 * c + 1, 0:rows] for c in range(own)]
        for number, (tiles, odd_only, chosen) in enumerate(((x, False, pairs), (y, True, pairs), (z, False, odds))):
            got = picked(paired(tiles, odd_only), chosen)
            for c in range(own):
                target[number, 4 + c, 0:half] = got[c * half:(c + 1) * half]

    coarse_faces(IN, 3, F1, 4, 32, pairs0, odds0)
    faces1, _ = exchange(F1, F1, F1S, 4, 16, 1)
    coarse_faces(F1, 4, F2, 2, 16, pairs1, odds1)
    near, later = exchange(F2, F2, F2S, 2, 8, 2)
    faces2 = near + later

    lane_block = iota((8, 128), 1) >> 5
    both_rows = (tile_row >> 1) == lane_block
    odd_rows = tile_row == 2 * lane_block + 1

    def to_row(tile, chosen, mask):
        got = jnp.where(mask, picked(tile, chosen), 0.0)
        return jnp.broadcast_to(jnp.sum(got, axis=0, keepdims=True), (narrow, 128))

    T3s[0] = to_row(F2[0, 5, 0:8], pairs2, both_rows)
    T3s[1] = to_row(F2[1, 4, 0:8] + F2[1, 5, 0:8], pairs2, odd_rows)
    T3s[2] = to_row(F2[2, 4, 0:8] + F2[2, 5, 0:8], odds2, both_rows)
    gather_f = [send(T3s, T3r.at[j], (i, narrow_at(d))) for d in range(1, narrow)]
    T3r[j] = T3s[...]

    arrive(first)
    has_low, has_high = j > 0, j < narrow - 1

    @pl.loop(0, 12)
    def unpack(q):
        low, high = RK[0, q], RK[1, q]
        for f in range(4):
            from_high = pltpu.roll(high, (8 - 2 * f) % 8, 0)
            from_low = pltpu.roll(low, (14 - 2 * f) % 8, 0)
            if f == 1:
                from_low = jnp.where(has_low, from_low, 0.0)
            IN[f, q + 1, 32:40] = jnp.where(row256 < 2, from_high, jnp.where(row256 >= 6, from_low, 0.0))

    IN[0, 0, 32:40] = jnp.zeros((8, 256), F32)
    for p in range(8):
        IN[1, 3 + p, 37:38] = jnp.where(has_low, FYr[p:p + 1], 0.0)

    @pl.when(i == 0)
    def _():
        IN[0, 2] = jnp.zeros((40, 256), F32)

    def inside(rows, lanes, own_rows, reach):
        row = iota((rows, lanes), 0)
        mask = (row < own_rows) | ((row < own_rows + reach) & has_high) | ((row >= rows - reach) & has_low)
        return mask

    def plane_in(p, own):
        return (i * own + p >= 0) & (i * own + p < own * wide)

    rows_in0 = inside(40, 256, 32, 2)
    weight_in = jnp.where(rows_in0, relax, 0.0)

    @pl.loop(-2, 10)
    def start0(p):
        w = jnp.where(plane_in(p, 8), weight_in, 0.0) / diagonal(IN, p + 3)
        W0[p + 3] = w
        VA[p + 3] = w * IN[3, p + 3]

    @pl.loop(-1, 9)
    def down0(p):
        VD[p + 3] = VA[p + 3] + W0[p + 3] * remainder(IN.at[3], IN, VA, p + 3)

    background = []
    background.append(send(VD.at[pl.ds(8, 3), pl.ds(0, 32)], VB.at[pl.ds(0, 3)], (wide_at(1), j)))
    background.append(send(VD.at[pl.ds(3, 3), pl.ds(0, 32)], VB.at[pl.ds(3, 3)], (wide_at(-1), j)))
    for side, b, row in ((0, 1, 24), (1, -1, 0)):
        background.append(send(VD.at[pl.ds(3, 8), pl.ds(row, 8)], VY.at[side, pl.ds(3, 8)], (i, narrow_at(b))))
        background.append(send(VD.at[pl.ds(8, 3), pl.ds(row, 8)], VY.at[side, pl.ds(0, 3)], (wide_at(1), narrow_at(b))))
        background.append(send(VD.at[pl.ds(3, 3), pl.ds(row, 8)], VY.at[side, pl.ds(11, 3)], (wide_at(-1), narrow_at(b))))

    @pl.loop(0, 4)
    def restrict0(c):
        VE[c, 0:32] = remainder(IN.at[3], IN, VD, 2 * c + 3)[:32] + remainder(IN.at[3], IN, VD, 2 * c + 4)[:32]

    got = paired([VE[c, 0:32] for c in range(4)])
    got = picked(got, pairs0)
    for c in range(4):
        B1[0, 4 + c, 0:16] = got[16 * c:16 * (c + 1)]
    rhs1, _ = exchange(B1, B1, B1S, 4, 16, 1)

    arrive(gather_f)
    sub = iota((narrow, 128), 0)

    def assembled(parts):
        tile = parts[0]
        for n in range(1, narrow):
            tile = jnp.where(sub == n, parts[n], tile)
        return tile

    for f in range(3):
        G3f[f, zi, ri] = assembled([T3r[n, f] for n in range(narrow)])
    gather_f = [send(G3f.at[:, zi, ri], G3f.at[:, zi, ri], (lax.rem(zi + d, ring) * group + ri, j)) for d in range(1, ring)]

    def finish_faces(f, stage, planes, rows):
        for p in range(planes):
            for field in range(3):
                tile = merged(stage, field, p)
                if field == 1:
                    tile = jnp.where((tile_row < 4) | has_low, tile, 0.0)
                f[field, p, rows:rows + 8] = tile

        @pl.when(i == 0)
        def _():
            f[0, 3] = jnp.zeros(f.shape[2:], F32)

        if planes == 10:
            @pl.when(i == 1)
            def _():
                f[0, 1] = jnp.zeros(f.shape[2:], F32)

    arrive(faces1)
    finish_faces(F1, F1S, 12, 16)
    rows_in1 = inside(24, 128, 16, 4)
    weight_in1 = jnp.where(rows_in1, relax, 0.0)

    @pl.loop(-3, 8)
    def weights1(p):
        W1[p + 4] = jnp.where(plane_in(p, 4), weight_in1, 0.0) / diagonal(F1, p + 4)

    arrive(rhs1)
    for p in range(12):
        B1[0, p, 16:24] = merged(B1S, 0, p)

    @pl.loop(-2, 6)
    def start1(p):
        X1[p + 4] = W1[p + 4] * B1[0, p + 4]

    @pl.loop(-1, 5)
    def down1(p):
        Y1[0, p + 4] = X1[p + 4] + W1[p + 4] * remainder(B1.at[0], F1, X1, p + 4)

    back1, _ = exchange(Y1, Y1R, Y1S, 4, 16, 1)
    got = paired([remainder(B1.at[0], F1, Y1.at[0], 2 * c + 4)[:16] + remainder(B1.at[0], F1, Y1.at[0], 2 * c + 5)[:16]
                  for c in range(2)])
    got = picked(got, pairs1)
    for c in range(2):
        B2[0, 4 + c, 0:8] = got[8 * c:8 * (c + 1)]
    rhs2, rhs2_far = exchange(B2, B2, B2S, 2, 8, 2)

    arrive(gather_f)
    gather_f = [send(G3f.at[:, :, ri], G3f.at[:, :, ri], (zi * group + lax.rem(ri + d, group), j)) for d in range(1, group)]

    arrive(faces2)
    finish_faces(F2, F2S, 10, 8)
    rows_in2 = inside(16, 128, 8, 4) & (iota((16, 128), 1) < 64)

    @pl.loop(-3, 6)
    def weights2(p):
        W2[p + 4] = jnp.where(rows_in2 & plane_in(p, 2), relax / diagonal(F2, p + 4), 0.0)

    arrive(rhs2)
    for p in range(2, 8):
        B2[0, p, 8:16] = merged(B2S, 0, p)

    for p in range(-2, 4):
        X2[p + 4] = W2[p + 4] * B2[0, p + 4]
    for p in range(-1, 3):
        Y2[0, p + 4] = X2[p + 4] + W2[p + 4] * remainder(B2.at[0], F2, X2, p + 4)
    back2_near, back2_far = exchange(Y2, Y2R, Y2S, 2, 8, 2)
    got = remainder(B2.at[0], F2, Y2.at[0], 4)[:8] + remainder(B2.at[0], F2, Y2.at[0], 5)[:8]
    B3s[...] = to_row(got, pairs2, both_rows)
    gather_b = [send(B3s, B3r.at[j], (i, narrow_at(d))) for d in range(1, narrow)]
    B3r[j] = B3s[...]
    arrive(gather_b)
    G3b[zi, ri] = assembled([B3r[n] for n in range(narrow)])
    gather_b = [send(G3b.at[zi, ri], G3b.at[zi, ri], (lax.rem(zi + d, ring) * group + ri, j)) for d in range(1, ring)]

    arrive(gather_f)
    block3 = iota((narrow, 128), 1) >> 5
    lane3 = iota((narrow, 128), 1) & 31
    last_y = (sub == narrow - 1) & (block3 == 3)
    last_lane = lane3 == 31

    @pl.loop(0, wide)
    def masks3(p):
        a, b = lax.div(p, group), lax.rem(p, group)
        y, z = G3f[1, a, b], G3f[2, a, b]
        EG[p] = jnp.where(last_y, y, 0.0) + jnp.where(last_lane, z, 0.0)
        YG[p] = jnp.where(last_y, 0.0, y)
        ZG[p] = jnp.where(last_lane, 0.0, z)

    arrive(gather_b)
    gather_b = [send(G3b.at[:, ri], G3b.at[:, ri], (zi * group + lax.rem(ri + d, group), j)) for d in range(1, group)]
    for p in (0, 1, wide + 2, wide + 3):
        PD[p] = jnp.zeros((narrow, 128), F32)
    for p in range(5):
        XS[p] = jnp.zeros((narrow, 128), F32)
    arrive(gather_b)

    zero3 = jnp.zeros((narrow, 128), F32)

    def next_y3(cells):
        moved = pltpu.roll(cells, 96, 1)
        return jnp.where(block3 == 3, pltpu.roll(moved, narrow - 1, 0), moved)

    def last_y3(cells):
        moved = pltpu.roll(cells, 32, 1)
        return jnp.where(block3 == 0, pltpu.roll(moved, 1, 0), moved)

    def begin(a, total):
        for b in range(group):
            p = a * group + b
            r = G3b[a, b]
            PD[p + 2] = r
            RR[p] = r
            total = total + r * r
        return total

    def summed(total):
        return jnp.sum(jnp.sum(total, axis=0, keepdims=True), axis=1, keepdims=True)

    def image(a, carry):
        total, low = carry
        for b in range(group):
            p = a * group + b
            here = PD[p + 2]
            high = G3f[0, a, b] * (here - PD[p + 3])
            along_y = YG[p] * (here - next_y3(here))
            along_z = ZG[p] * (here - pltpu.roll(here, 127, 1))
            q = (EG[p] * here + (high - low)) + ((along_y - last_y3(along_y)) + (along_z - pltpu.roll(along_z, 1, 1)))
            QQ[p] = q
            total = total + here * q
            low = high
        return total, low

    norm_now = summed(lax.fori_loop(0, ring, begin, zero3))
    for counter in range(CGI):
        total, _ = lax.fori_loop(0, ring, image, (zero3, zero3))
        alpha = norm_now / summed(total)
        for p in range(5):
            XS[p] = XS[p] + alpha * PD[i + p]
        if counter == CGI - 1:
            break

        def descend(a, total, alpha=alpha):
            for b in range(group):
                p = a * group + b
                r = RR[p] - alpha * QQ[p]
                RR[p] = r
                total = total + r * r
            return total

        norm_next = summed(lax.fori_loop(0, ring, descend, zero3))
        beta = norm_next / norm_now

        def turn(a, carry, beta=beta):
            for b in range(group):
                p = a * group + b
                PD[p + 2] = RR[p] + beta * PD[p + 2]
            return carry

        lax.fori_loop(0, ring, turn, 0)
        norm_now = norm_next

    row16 = iota((16, 128), 0)
    wanted = ((row16 & 7) >> 1) == (iota((16, 128), 1) >> 5)
    spread2 = ones_where(((iota((128, 128), 1) >> 1) == (iota((128, 128), 0) & 31)) & (iota((128, 128), 1) < 64))
    high_j, low_j = jnp.minimum(j + 1, narrow - 1), jnp.maximum(j - 1, 0)
    spread = []
    for p in range(5):
        middle = jnp.broadcast_to(XS[p, pl.ds(j, 1), :], (16, 128))
        above = jnp.broadcast_to(XS[p, pl.ds(high_j, 1), :], (16, 128))
        below = jnp.broadcast_to(XS[p, pl.ds(low_j, 1), :], (16, 128))
        x = jnp.where(row16 < 8, middle, jnp.where(row16 < 12, above, below))
        spread.append(jnp.where(wanted, x, 0.0))
    spread = picked(jnp.concatenate(spread, axis=0), spread2)
    arrive(rhs2_far + back2_near + back2_far)
    reach2 = inside(16, 128, 8, 4)
    for p in (0, 1, 8, 9):
        B2[0, p, 8:16] = merged(B2S, 0, p)
    for p in range(-4, 6):
        own = Y2[0, p + 4, 0:8] if 0 <= p < 2 else Y2R[0, p + 4, 0:8]
        x = jnp.concatenate([own, merged(Y2S, 0, p + 4)], axis=0)
        c = (p + 4) // 2
        x = x + spread[16 * c:16 * (c + 1)]
        X2[p + 4] = jnp.where(reach2 & plane_in(p, 2), x, 0.0)
    for p in range(-3, 5):
        Z2[p + 4] = X2[p + 4] + W2[p + 4] * remainder(B2.at[0], F2, X2, p + 4)
    for p in range(-2, 4):
        X2[p + 4] = Z2[p + 4] + W2[p + 4] * remainder(B2.at[0], F2, Z2, p + 4)

    spread1 = ones_where((iota((128, 128), 1) >> 1) == iota((128, 128), 0))
    spread = picked(jnp.concatenate([X2[p + 4] for p in range(-2, 4)], axis=0), spread1)
    for c in range(6):
        U1[c, pl.ds(0, 16, stride=2), :] = spread[16 * c:16 * (c + 1)]
        U1[c, pl.ds(1, 16, stride=2), :] = spread[16 * c:16 * (c + 1)]
    arrive(back1)
    reach1 = inside(24, 128, 16, 4)
    for p in range(-4, 8):
        c = (p + 4) // 2
        own = Y1[0, p + 4, 0:16] if 0 <= p < 4 else Y1R[0, p + 4, 0:16]
        edge = merged(Y1S, 0, p + 4) + jnp.where(tile_row < 4, U1[c, 16:24], U1[c, 24:32])
        x = jnp.concatenate([own + U1[c, 0:16], edge], axis=0)
        X1[p + 4] = jnp.where(reach1 & plane_in(p, 4), x, 0.0)

    @pl.loop(-3, 7)
    def up1(p):
        Z1[p + 4] = X1[p + 4] + W1[p + 4] * remainder(B1.at[0], F1, X1, p + 4)

    @pl.loop(-2, 6)
    def up1_again(p):
        X1[p + 4] = Z1[p + 4] + W1[p + 4] * remainder(B1.at[0], F1, Z1, p + 4)

    spread0 = ones_where((iota((128, 256), 1) >> 1) == iota((128, 256), 0))
    spread = picked(jnp.concatenate([X1[p + 4] for p in range(-2, 6)], axis=0), spread0)
    for c in range(8):
        for half in (0, 128):
            part = spread[24 * c:24 * (c + 1), half:half + 128]
            U0[half // 128, c, pl.ds(0, 24, stride=2), :] = part
            U0[half // 128, c, pl.ds(1, 24, stride=2), :] = part
    arrive(background)
    reach0 = inside(40, 256, 32, 4)

    def corrected(p, own):
        c = lax.div(p + 4, 2)
        u = jnp.concatenate([U0[0, c], U0[1, c]], axis=1)
        edge = jnp.where(row256 < 4, VY[1, p + 3] + u[32:40], VY[0, p + 3] + u[40:48])
        x = jnp.concatenate([own + u[0:32], edge], axis=0)
        return jnp.where(reach0 & plane_in(p, 8), x, 0.0)

    @pl.loop(0, 8)
    def correct0(p):
        VE[p + 3] = corrected(p, VD[p + 3, 0:32])

    @pl.loop(0, 3)
    def correct0_ends(p):
        VE[p] = corrected(p - 3, VB[p])
        VE[p + 11] = corrected(p + 8, VB[p + 3])

    @pl.loop(-2, 10)
    def up0(p):
        VA[p + 3] = VE[p + 3] + W0[p + 3] * remainder(IN.at[3], IN, VE, p + 3)

    @pl.loop(-1, 9)
    def up0_again(p):
        VF[p + 3] = VA[p + 3] + W0[p + 3] * remainder(IN.at[3], IN, VA, p + 3)

    store = pltpu.make_async_copy(VF.at[pl.ds(3, 8), pl.ds(0, 32)], out_p, store_sem.at[0])
    store.start()

    @pl.loop(0, 8)
    def rest0(p):
        VE[p] = remainder(IN.at[3], IN, VF, p + 3)

    store_r = pltpu.make_async_copy(VE.at[pl.ds(0, 8), pl.ds(0, 32)], out_r, store_sem.at[1])
    store_r.start()
    for copy in sent:
        copy.wait_send()
    store.wait()
    store_r.wait()


def shards(sizes, source, face_x, face_y, face_z):
    wide, narrow, ring, group = sizes
    shape = jax.ShapeDtypeStruct((8, 32, 256), F32)

    def V(*size):
        return pltpu.VMEM(size, F32)

    scratch = [
        V(4, 13, 40, 256), V(2, 8, 8, 256), V(8, 256), V(8, 256), V(2, 12, 8, 256),
        V(14, 40, 256), V(14, 40, 256), V(14, 40, 256), V(6, 32, 256), V(2, 14, 8, 256), V(14, 40, 256), V(14, 40, 256),
        V(2, 4, 32, 128), V(2, 8, 48, 128),
        V(3, 12, 24, 128), V(2, 3, 12, 8, 128), V(1, 12, 24, 128), V(2, 1, 12, 8, 128), V(12, 24, 128), V(12, 24, 128),
        V(1, 12, 24, 128), V(1, 12, 24, 128), V(2, 1, 12, 8, 128), V(12, 24, 128), V(6, 32, 128),
        V(3, 10, 16, 128), V(2, 3, 10, 8, 128), V(1, 10, 16, 128), V(2, 1, 10, 8, 128), V(10, 16, 128), V(10, 16, 128),
        V(1, 10, 16, 128), V(1, 10, 16, 128), V(2, 1, 10, 8, 128), V(10, 16, 128),
        V(3, narrow, 128), V(narrow, 3, narrow, 128), V(3, ring, group, narrow, 128),
        V(narrow, 128), V(narrow, narrow, 128), V(ring, group, narrow, 128), V(wide, narrow, 128),
        V(wide, narrow, 128), V(wide, narrow, 128),
        V(wide + 4, narrow, 128), V(wide, narrow, 128), V(wide, narrow, 128), V(5, narrow, 128),
        pltpu.SemaphoreType.DMA((144,)), pltpu.SemaphoreType.DMA((144,)), pltpu.SemaphoreType.DMA((4,)),
        pltpu.SemaphoreType.DMA((2,)),
    ]
    anywhere = pl.BlockSpec(memory_space=pl.ANY)
    return pl.pallas_call(
        functools.partial(body, sizes),
        out_shape=(shape, shape),
        in_specs=[anywhere] * 4,
        out_specs=(anywhere, anywhere),
        scratch_shapes=scratch,
        compiler_params=pltpu.CompilerParams(collective_id=0, has_side_effects=True, vmem_limit_bytes=40 * 1024 * 1024),
    )(source, face_x, face_y, face_z)


def solution(mesh):
    wide, narrow = mesh.shape["wide"], mesh.shape["narrow"]
    group = 8 if wide == 64 else wide // 2
    spec = P("wide", "narrow", None)
    return jax.shard_map(
        functools.partial(shards, (wide, narrow, wide // group, group)),
        mesh=mesh,
        in_specs=(spec,) * 4,
        out_specs=(spec, spec),
        check_vma=False,
    )
```

time: 1850 us -> 80.1 us (0.04)
  the two profiles are of different devices: /device:TPU:199 before, /device:TPU:1 now
where the time goes in v1:
time: 80.1 us; the launch traced here: 79.5 us
  Pallas kernels  73.7 us (92%)
  local copies, waits for them, and re-layouts  5.2 us (6%)
    pallas_call x1, Pallas kernels, shards(): pl.pallas_call(functools.partial(body, sizes), out_shape=(shape, shape),...  73.7 us
    unnamed x10, local copies, waits for them, and re-layouts  5.2 us

profile of v1, /device:TPU:1, one launch (start us, length us, event | category | flops | bytes accessed | tf_op | source)
XLA Modules:
  0.0 79.5 jit_solution(769674086481889890)
XLA Ops:
  0.6 0.0 copy-start
  0.6 0.9 %copy-done = f32[8,32,256]{2,1,0:T(8,128)S(1)} copy-done((f32[8,32,256]{2,1,0:T(8,128)S(1)}, f32[8,32,256]{2,1,0:T(8,128)}, u32[]{:S(2)}) %copy-start) | copy-done | bytes 262168
  1.6 0.0 copy-start.1
  1.6 0.9 %copy-done.1 = f32[8,32,256]{2,1,0:T(8,128)S(1)} copy-done((f32[8,32,256]{2,1,0:T(8,128)S(1)}, f32[8,32,256]{2,1,0:T(8,128)}, u32[]{:S(2)}) %copy-start.1) | copy-done | bytes 262168
  2.5 0.0 copy-start.2
  2.5 0.9 %copy-done.2 = f32[8,32,256]{2,1,0:T(8,128)S(1)} copy-done((f32[8,32,256]{2,1,0:T(8,128)S(1)}, f32[8,32,256]{2,1,0:T(8,128)}, u32[]{:S(2)}) %copy-start.2) | copy-done | bytes 262168
  3.5 0.0 copy-start.3
  3.5 0.9 %copy-done.3 = f32[8,32,256]{2,1,0:T(8,128)S(1)} copy-done((f32[8,32,256]{2,1,0:T(8,128)S(1)}, f32[8,32,256]{2,1,0:T(8,128)}, u32[]{:S(2)}) %copy-start.3) | copy-done | bytes 262168
  4.4 73.7 %shard_map.59 = (f32[8,32,256]{2,1,0:T(8,128)S(1)}, f32[8,32,256]{2,1,0:T(8,128)S(1)}) custom-call(f32[8,32,256]{2,1,0:T(8,128)S(1)} %copy-done, f32[8,32,256]{2,1,0:T(8,128)S(1)} %copy-done.1, f32[8,32,256]{2,1,0:T(8,128)S(1)} %copy-done.2, f32[8,32,256]{2,1,0:T(8,128)S(1)} %copy-done.3), custom_call_target="tpu_custom_call" | custom-call | tf_op jit(solution)/shard_map/pallas_call | solution.py:574
  78.1 0.7 copy.8
  78.8 0.7 copy.9
Async XLA Ops:
  0.6 1.0 %copy-start = (f32[8,32,256]{2,1,0:T(8,128)S(1)}, f32[8,32,256]{2,1,0:T(8,128)}, u32[]{:S(2)}) copy-start(f32[8,32,256]{2,1,0:T(8,128)} %src.1) | copy-start | bytes 786436
  1.6 0.9 %copy-start.1 = (f32[8,32,256]{2,1,0:T(8,128)S(1)}, f32[8,32,256]{2,1,0:T(8,128)}, u32[]{:S(2)}) copy-start(f32[8,32,256]{2,1,0:T(8,128)} %inx.1) | copy-start | bytes 786436
  2.5 0.9 %copy-start.2 = (f32[8,32,256]{2,1,0:T(8,128)S(1)}, f32[8,32,256]{2,1,0:T(8,128)}, u32[]{:S(2)}) copy-start(f32[8,32,256]{2,1,0:T(8,128)} %iny.1) | copy-start | bytes 786436
  3.5 0.9 %copy-start.3 = (f32[8,32,256]{2,1,0:T(8,128)S(1)}, f32[8,32,256]{2,1,0:T(8,128)}, u32[]{:S(2)}) copy-start(f32[8,32,256]{2,1,0:T(8,128)} %inz.1) | copy-start | bytes 786436

commit v2 on v1

--- a/solution.py
+++ b/solution.py
@@ -53,24 +53,29 @@
     return jnp.concatenate([jnp.where(lane == 0, 0.0, first), jnp.where(lane == 0, first, second)], axis=axis)
 
 
-def remainder(b, f, v, p):
-    here = v[p]
-    rows = here.shape[0]
-    flow = f[0, p] * (v[p + 1] - here) - f[0, p - 1] * (here - v[p - 1])
-    along = f[1, p] * (pltpu.roll(here, rows - 1, 0) - here)
-    flow = flow + (along - pltpu.roll(along, 1, 0))
-    along = f[2, p] * (next_z(here) - here)
+def remainder(b, f, v, p, n=1):
+    here = v[pl.ds(p, n)]
+    rows = here.shape[1]
+    flow = f[0, pl.ds(p, n)] * (v[pl.ds(p + 1, n)] - here) - f[0, pl.ds(p - 1, n)] * (here - v[pl.ds(p - 1, n)])
+    along = f[1, pl.ds(p, n)] * (pltpu.roll(here, rows - 1, 1) - here)
+    flow = flow + (along - pltpu.roll(along, 1, 1))
+    along = f[2, pl.ds(p, n)] * (next_z(here) - here)
     flow = flow + (along - last_z(along))
-    return b[p] + flow
-
-
-def diagonal(f, p):
-    return (f[0, p] + f[0, p - 1]) + (f[1, p] + pltpu.roll(f[1, p], 1, 0)) + (f[2, p] + last_z(f[2, p]))
+    return b[pl.ds(p, n)] + flow
+
+
+def diagonal(f, p, n=1):
+    x, y, z = f[0, pl.ds(p, n)], f[1, pl.ds(p, n)], f[2, pl.ds(p, n)]
+    return (x + f[0, pl.ds(p - 1, n)]) + (y + pltpu.roll(y, 1, 1)) + (z + last_z(z))
+
+
+def sweep(target, v, b, f, w, p, n):
+    target[pl.ds(p, n)] = v[pl.ds(p, n)] + w[pl.ds(p, n)] * remainder(b, f, v, p, n)
 
 
 def body(sizes, src, inx, iny, inz, out_p, out_r, IN, PKs, FYs, FYr, RK, W0, VA, VD, VB, VY, VE, VF, RZ, U0,
          F1, F1S, B1, B1S, W1, X1, Y1, Y1R, Y1S, Z1, U1, F2, F2S, B2, B2S, W2, X2, Y2, Y2R, Y2S, Z2,
-         T3s, T3r, G3f, B3s, B3r, G3b, EG, YG, ZG, PD, RR, QQ, XS, send_sem, recv_sem, load_sem, store_sem):
+         T3s, T3r, G3f, B3s, B3r, G3b, EG, XG, YG, ZG, PD, RR, QQ, XS, send_sem, recv_sem, load_sem, store_sem):
     wide, narrow, ring, group = sizes
     i, j = lax.axis_index("wide"), lax.axis_index("narrow")
     zi, ri = lax.div(i, group), lax.rem(i, group)
@@ -87,7 +92,7 @@
         loads[-1].start()
 
     barrier = pltpu.get_barrier_semaphore()
-    partners = [(wide_at(a), narrow_at(b)) for a in range(-2, 3) for b in range(-1, 2) if (a, b) != (0, 0)]
+    partners = [(wide_at(a), narrow_at(b)) for a in (0, 1, -1, 2, -2) for b in (0, 1, -1) if (a, b) != (0, 0)]
     partners += [(i, narrow_at(d)) for d in range(2, narrow - 1)]
     partners += [(lax.rem(zi + d, ring) * group + ri, j) for d in range(1, ring)]
     partners += [(zi * group + lax.rem(ri + d, group), j) for d in range(1, group)]
@@ -135,34 +140,37 @@
     def merged(stage, field, plane):
         return jnp.where(tile_row < 4, stage[1, field, plane], stage[0, field, plane])
 
+    pl.semaphore_wait(barrier, len(partners))
+    first = []
+    for number, ref in enumerate((inx, iny, inz, src)):
+        more = 3 if number == 0 else 2
+        first.append(send(ref.at[pl.ds(8 - more, more)], IN.at[number, pl.ds(3 - more, more), pl.ds(0, 32)], (wide_at(1), j)))
+        first.append(send(ref.at[pl.ds(0, 2)], IN.at[number, pl.ds(11, 2), pl.ds(0, 32)], (wide_at(-1), j)))
+
     for copy in loads:
         copy.wait()
 
-    @pl.loop(0, 8)
-    def pack(p):
-        up = jnp.zeros((8, 256), F32)
-        down = jnp.zeros((8, 256), F32)
-        for f in range(4):
-            mine = (row256 >> 1) == f
-            up = jnp.where(mine, pltpu.roll(IN[f, 3 + p, 24:32], (2 * f + 2) % 8, 0), up)
-            down = jnp.where(mine, pltpu.roll(IN[f, 3 + p, 0:8], 2 * f, 0), down)
-        PKs[0, p] = up
-        PKs[1, p] = down
+    @pl.loop(0, 4)
+    def pack(c):
+        for p in (2 * c, 2 * c + 1):
+            up = jnp.zeros((8, 256), F32)
+            down = jnp.zeros((8, 256), F32)
+            for f in range(4):
+                mine = (row256 >> 1) == f
+                up = jnp.where(mine, pltpu.roll(IN[f, 3 + p, 24:32], (2 * f + 2) % 8, 0), up)
+                down = jnp.where(mine, pltpu.roll(IN[f, 3 + p, 0:8], 2 * f, 0), down)
+            PKs[0, p] = up
+            PKs[1, p] = down
 
     for p in range(8):
         FYs[p:p + 1] = IN[1, 3 + p, 29:30]
 
-    pl.semaphore_wait(barrier, len(partners))
-
-    first = []
-    first.append(send(IN.at[:, pl.ds(9, 2), pl.ds(0, 32)], IN.at[:, pl.ds(1, 2), pl.ds(0, 32)], (wide_at(1), j)))
-    first.append(send(IN.at[:, pl.ds(3, 2), pl.ds(0, 32)], IN.at[:, pl.ds(11, 2), pl.ds(0, 32)], (wide_at(-1), j)))
-    first.append(send(IN.at[0, pl.ds(8, 1), pl.ds(0, 32)], IN.at[0, pl.ds(0, 1), pl.ds(0, 32)], (wide_at(1), j)))
     for side, b in ((0, 1), (1, -1)):
         first.append(send(PKs.at[side], RK.at[side, pl.ds(2, 8)], (i, narrow_at(b))))
+    first.append(send(FYs, FYr, (i, narrow_at(1))))
+    for side, b in ((0, 1), (1, -1)):
         first.append(send(PKs.at[side, pl.ds(6, 2)], RK.at[side, pl.ds(0, 2)], (wide_at(1), narrow_at(b))))
         first.append(send(PKs.at[side, pl.ds(0, 2)], RK.at[side, pl.ds(10, 2)], (wide_at(-1), narrow_at(b))))
-    first.append(send(FYs, FYr, (i, narrow_at(1))))
 
     pairs0 = ones_where((iota((256, 128), 0) >> 1) == iota((256, 128), 1))
     odds0 = ones_where(iota((256, 128), 0) == 2 * iota((256, 128), 1) + 1)
@@ -248,15 +256,16 @@
     rows_in0 = inside(40, 256, 32, 2)
     weight_in = jnp.where(rows_in0, relax, 0.0)
 
-    @pl.loop(-2, 10)
-    def start0(p):
-        w = jnp.where(plane_in(p, 8), weight_in, 0.0) / diagonal(IN, p + 3)
-        W0[p + 3] = w
-        VA[p + 3] = w * IN[3, p + 3]
-
-    @pl.loop(-1, 9)
-    def down0(p):
-        VD[p + 3] = VA[p + 3] + W0[p + 3] * remainder(IN.at[3], IN, VA, p + 3)
+    @pl.loop(-1, 5)
+    def start0(c):
+        p = 2 * c
+        w = jnp.where(plane_in(p, 8), weight_in, 0.0)[None] / diagonal(IN, p + 3, 2)
+        W0[pl.ds(p + 3, 2)] = w
+        VA[pl.ds(p + 3, 2)] = w * IN[3, pl.ds(p + 3, 2)]
+
+    @pl.loop(0, 5)
+    def down0(c):
+        sweep(VD, VA, IN.at[3], IN, W0, 2 * c + 2, 2)
 
     background = []
     background.append(send(VD.at[pl.ds(8, 3), pl.ds(0, 32)], VB.at[pl.ds(0, 3)], (wide_at(1), j)))
@@ -268,7 +277,8 @@
 
     @pl.loop(0, 4)
     def restrict0(c):
-        VE[c, 0:32] = remainder(IN.at[3], IN, VD, 2 * c + 3)[:32] + remainder(IN.at[3], IN, VD, 2 * c + 4)[:32]
+        both = remainder(IN.at[3], IN, VD, 2 * c + 3, 2)
+        VE[c, 0:32] = both[0, :32] + both[1, :32]
 
     got = paired([VE[c, 0:32] for c in range(4)])
     got = picked(got, pairs0)
@@ -290,12 +300,11 @@
     gather_f = [send(G3f.at[:, zi, ri], G3f.at[:, zi, ri], (lax.rem(zi + d, ring) * group + ri, j)) for d in range(1, ring)]
 
     def finish_faces(f, stage, planes, rows):
-        for p in range(planes):
-            for field in range(3):
-                tile = merged(stage, field, p)
-                if field == 1:
-                    tile = jnp.where((tile_row < 4) | has_low, tile, 0.0)
-                f[field, p, rows:rows + 8] = tile
+        for field in range(3):
+            tile = jnp.where(tile_row[None] < 4, stage[1, field], stage[0, field])
+            if field == 1:
+                tile = jnp.where(((tile_row < 4) | has_low)[None], tile, 0.0)
+            f[field, :, rows:rows + 8] = tile
 
         @pl.when(i == 0)
         def _():
@@ -311,25 +320,18 @@
     rows_in1 = inside(24, 128, 16, 4)
     weight_in1 = jnp.where(rows_in1, relax, 0.0)
 
-    @pl.loop(-3, 8)
-    def weights1(p):
-        W1[p + 4] = jnp.where(plane_in(p, 4), weight_in1, 0.0) / diagonal(F1, p + 4)
+    for p, n in ((-3, 3), (0, 4), (4, 4)):
+        W1[p + 4:p + 4 + n] = jnp.where(plane_in(p, 4), weight_in1, 0.0)[None] / diagonal(F1, p + 4, n)
 
     arrive(rhs1)
-    for p in range(12):
-        B1[0, p, 16:24] = merged(B1S, 0, p)
-
-    @pl.loop(-2, 6)
-    def start1(p):
-        X1[p + 4] = W1[p + 4] * B1[0, p + 4]
-
-    @pl.loop(-1, 5)
-    def down1(p):
-        Y1[0, p + 4] = X1[p + 4] + W1[p + 4] * remainder(B1.at[0], F1, X1, p + 4)
+    B1[0, :, 16:24] = jnp.where(tile_row[None] < 4, B1S[1, 0], B1S[0, 0])
+    X1[2:10] = W1[2:10] * B1[0, 2:10]
+    for p in (-1, 2):
+        sweep(Y1.at[0], X1, B1.at[0], F1, W1, p + 4, 3)
 
     back1, _ = exchange(Y1, Y1R, Y1S, 4, 16, 1)
-    got = paired([remainder(B1.at[0], F1, Y1.at[0], 2 * c + 4)[:16] + remainder(B1.at[0], F1, Y1.at[0], 2 * c + 5)[:16]
-                  for c in range(2)])
+    rest = remainder(B1.at[0], F1, Y1.at[0], 4, 4)
+    got = paired([rest[2 * c, :16] + rest[2 * c + 1, :16] for c in range(2)])
     got = picked(got, pairs1)
     for c in range(2):
         B2[0, 4 + c, 0:8] = got[8 * c:8 * (c + 1)]
@@ -342,21 +344,17 @@
     finish_faces(F2, F2S, 10, 8)
     rows_in2 = inside(16, 128, 8, 4) & (iota((16, 128), 1) < 64)
 
-    @pl.loop(-3, 6)
-    def weights2(p):
-        W2[p + 4] = jnp.where(rows_in2 & plane_in(p, 2), relax / diagonal(F2, p + 4), 0.0)
+    weights = relax / diagonal(F2, 1, 9)
+    for p in range(-3, 6):
+        W2[p + 4] = jnp.where(rows_in2 & plane_in(p, 2), weights[p + 3], 0.0)
 
     arrive(rhs2)
-    for p in range(2, 8):
-        B2[0, p, 8:16] = merged(B2S, 0, p)
-
-    for p in range(-2, 4):
-        X2[p + 4] = W2[p + 4] * B2[0, p + 4]
-    for p in range(-1, 3):
-        Y2[0, p + 4] = X2[p + 4] + W2[p + 4] * remainder(B2.at[0], F2, X2, p + 4)
+    B2[0, 2:8, 8:16] = jnp.where(tile_row[None] < 4, B2S[1, 0, 2:8], B2S[0, 0, 2:8])
+    X2[2:8] = W2[2:8] * B2[0, 2:8]
+    sweep(Y2.at[0], X2, B2.at[0], F2, W2, 3, 4)
     back2_near, back2_far = exchange(Y2, Y2R, Y2S, 2, 8, 2)
-    got = remainder(B2.at[0], F2, Y2.at[0], 4)[:8] + remainder(B2.at[0], F2, Y2.at[0], 5)[:8]
-    B3s[...] = to_row(got, pairs2, both_rows)
+    rest = remainder(B2.at[0], F2, Y2.at[0], 4, 2)
+    B3s[...] = to_row(rest[0, :8] + rest[1, :8], pairs2, both_rows)
     gather_b = [send(B3s, B3r.at[j], (i, narrow_at(d))) for d in range(1, narrow)]
     B3r[j] = B3s[...]
     arrive(gather_b)
@@ -369,13 +367,16 @@
     last_y = (sub == narrow - 1) & (block3 == 3)
     last_lane = lane3 == 31
 
-    @pl.loop(0, wide)
-    def masks3(p):
-        a, b = lax.div(p, group), lax.rem(p, group)
-        y, z = G3f[1, a, b], G3f[2, a, b]
-        EG[p] = jnp.where(last_y, y, 0.0) + jnp.where(last_lane, z, 0.0)
-        YG[p] = jnp.where(last_y, 0.0, y)
-        ZG[p] = jnp.where(last_lane, 0.0, z)
+    XG[0] = jnp.zeros((narrow, 128), F32)
+
+    @pl.loop(0, ring)
+    def masks3(a):
+        y, z = G3f[1, a], G3f[2, a]
+        planes = pl.ds(a * group, group)
+        XG[pl.ds(a * group + 1, group)] = G3f[0, a]
+        EG[planes] = jnp.where(last_y[None], y, 0.0) + jnp.where(last_lane[None], z, 0.0)
+        YG[planes] = jnp.where(last_y[None], 0.0, y)
+        ZG[planes] = jnp.where(last_lane[None], 0.0, z)
 
     arrive(gather_b)
     gather_b = [send(G3b.at[:, ri], G3b.at[:, ri], (zi * group + lax.rem(ri + d, group), j)) for d in range(1, group)]
@@ -385,70 +386,63 @@
         XS[p] = jnp.zeros((narrow, 128), F32)
     arrive(gather_b)
 
-    zero3 = jnp.zeros((narrow, 128), F32)
-
     def next_y3(cells):
-        moved = pltpu.roll(cells, 96, 1)
-        return jnp.where(block3 == 3, pltpu.roll(moved, narrow - 1, 0), moved)
+        moved = pltpu.roll(cells, 96, 2)
+        return jnp.where(block3[None] == 3, pltpu.roll(moved, narrow - 1, 1), moved)
 
     def last_y3(cells):
-        moved = pltpu.roll(cells, 32, 1)
-        return jnp.where(block3 == 0, pltpu.roll(moved, 1, 0), moved)
-
-    def begin(a, total):
-        for b in range(group):
-            p = a * group + b
-            r = G3b[a, b]
-            PD[p + 2] = r
-            RR[p] = r
-            total = total + r * r
-        return total
+        moved = pltpu.roll(cells, 32, 2)
+        return jnp.where(block3[None] == 0, pltpu.roll(moved, 1, 1), moved)
 
     def summed(total):
         return jnp.sum(jnp.sum(total, axis=0, keepdims=True), axis=1, keepdims=True)
 
-    def image(a, carry):
-        total, low = carry
-        for b in range(group):
-            p = a * group + b
-            here = PD[p + 2]
-            high = G3f[0, a, b] * (here - PD[p + 3])
-            along_y = YG[p] * (here - next_y3(here))
-            along_z = ZG[p] * (here - pltpu.roll(here, 127, 1))
-            q = (EG[p] * here + (high - low)) + ((along_y - last_y3(along_y)) + (along_z - pltpu.roll(along_z, 1, 1)))
-            QQ[p] = q
-            total = total + here * q
-            low = high
-        return total, low
-
-    norm_now = summed(lax.fori_loop(0, ring, begin, zero3))
-    for counter in range(CGI):
-        total, _ = lax.fori_loop(0, ring, image, (zero3, zero3))
-        alpha = norm_now / summed(total)
+    zero3 = jnp.zeros((narrow, 128), F32)
+    total = zero3
+    for a in range(ring):
+        r = G3b[a]
+        PD[2 + a * group:2 + (a + 1) * group] = r
+        RR[a * group:(a + 1) * group] = r
+        total = total + jnp.sum(r * r, axis=0)
+    norm_first = summed(total)
+
+    def curvature(keep):
+        total = zero3
+        for a in range(ring):
+            p = a * group
+            here = PD[p + 2:p + 2 + group]
+            high = XG[p + 1:p + 1 + group] * (here - PD[p + 3:p + 3 + group])
+            low = XG[p:p + group] * (PD[p + 1:p + 1 + group] - here)
+            along_y = YG[p:p + group] * (here - next_y3(here))
+            along_z = ZG[p:p + group] * (here - pltpu.roll(here, 127, 2))
+            q = (EG[p:p + group] * here + (high - low)) + (
+                (along_y - last_y3(along_y)) + (along_z - pltpu.roll(along_z, 1, 2)))
+            if keep:
+                QQ[p:p + group] = q
+            total = total + jnp.sum(here * q, axis=0)
+        return summed(total)
+
+    def iteration(counter, norm_now):
+        alpha = norm_now / curvature(True)
         for p in range(5):
             XS[p] = XS[p] + alpha * PD[i + p]
-        if counter == CGI - 1:
-            break
-
-        def descend(a, total, alpha=alpha):
-            for b in range(group):
-                p = a * group + b
-                r = RR[p] - alpha * QQ[p]
-                RR[p] = r
-                total = total + r * r
-            return total
-
-        norm_next = summed(lax.fori_loop(0, ring, descend, zero3))
+        total = zero3
+        for a in range(ring):
+            planes = slice(a * group, (a + 1) * group)
+            r = RR[planes] - alpha * QQ[planes]
+            RR[planes] = r
+            total = total + jnp.sum(r * r, axis=0)
+        norm_next = summed(total)
         beta = norm_next / norm_now
-
-        def turn(a, carry, beta=beta):
-            for b in range(group):
-                p = a * group + b
-                PD[p + 2] = RR[p] + beta * PD[p + 2]
-            return carry
-
-        lax.fori_loop(0, ring, turn, 0)
-        norm_now = norm_next
+        for a in range(ring):
+            p = a * group
+            PD[p + 2:p + 2 + group] = RR[p:p + group] + beta * PD[p + 2:p + 2 + group]
+        return norm_next
+
+    norm_now = lax.fori_loop(0, CGI - 1, iteration, norm_first)
+    alpha = norm_now / curvature(False)
+    for p in range(5):
+        XS[p] = XS[p] + alpha * PD[i + p]
 
     row16 = iota((16, 128), 0)
     wanted = ((row16 & 7) >> 1) == (iota((16, 128), 1) >> 5)
@@ -472,10 +466,8 @@
         c = (p + 4) // 2
         x = x + spread[16 * c:16 * (c + 1)]
         X2[p + 4] = jnp.where(reach2 & plane_in(p, 2), x, 0.0)
-    for p in range(-3, 5):
-        Z2[p + 4] = X2[p + 4] + W2[p + 4] * remainder(B2.at[0], F2, X2, p + 4)
-    for p in range(-2, 4):
-        X2[p + 4] = Z2[p + 4] + W2[p + 4] * remainder(B2.at[0], F2, Z2, p + 4)
+    sweep(Z2, X2, B2.at[0], F2, W2, 1, 8)
+    sweep(X2, Z2, B2.at[0], F2, W2, 2, 6)
 
     spread1 = ones_where((iota((128, 128), 1) >> 1) == iota((128, 128), 0))
     spread = picked(jnp.concatenate([X2[p + 4] for p in range(-2, 4)], axis=0), spread1)
@@ -491,13 +483,10 @@
         x = jnp.concatenate([own + U1[c, 0:16], edge], axis=0)
         X1[p + 4] = jnp.where(reach1 & plane_in(p, 4), x, 0.0)
 
-    @pl.loop(-3, 7)
-    def up1(p):
-        Z1[p + 4] = X1[p + 4] + W1[p + 4] * remainder(B1.at[0], F1, X1, p + 4)
-
-    @pl.loop(-2, 6)
-    def up1_again(p):
-        X1[p + 4] = Z1[p + 4] + W1[p + 4] * remainder(B1.at[0], F1, Z1, p + 4)
+    for p in (-3, 2):
+        sweep(Z1, X1, B1.at[0], F1, W1, p + 4, 5)
+    for p in (-2, 2):
+        sweep(X1, Z1, B1.at[0], F1, W1, p + 4, 4)
 
     spread0 = ones_where((iota((128, 256), 1) >> 1) == iota((128, 256), 0))
     spread = picked(jnp.concatenate([X1[p + 4] for p in range(-2, 6)], axis=0), spread0)
@@ -525,20 +514,20 @@
         VE[p] = corrected(p - 3, VB[p])
         VE[p + 11] = corrected(p + 8, VB[p + 3])
 
-    @pl.loop(-2, 10)
-    def up0(p):
-        VA[p + 3] = VE[p + 3] + W0[p + 3] * remainder(IN.at[3], IN, VE, p + 3)
-
-    @pl.loop(-1, 9)
-    def up0_again(p):
-        VF[p + 3] = VA[p + 3] + W0[p + 3] * remainder(IN.at[3], IN, VA, p + 3)
+    @pl.loop(0, 6)
+    def up0(c):
+        sweep(VA, VE, IN.at[3], IN, W0, 2 * c + 1, 2)
+
+    @pl.loop(0, 5)
+    def up0_again(c):
+        sweep(VF, VA, IN.at[3], IN, W0, 2 * c + 2, 2)
 
     store = pltpu.make_async_copy(VF.at[pl.ds(3, 8), pl.ds(0, 32)], out_p, store_sem.at[0])
     store.start()
 
-    @pl.loop(0, 8)
-    def rest0(p):
-        VE[p] = remainder(IN.at[3], IN, VF, p + 3)
+    @pl.loop(0, 4)
+    def rest0(c):
+        VE[pl.ds(2 * c, 2)] = remainder(IN.at[3], IN, VF, 2 * c + 3, 2)
 
     store_r = pltpu.make_async_copy(VE.at[pl.ds(0, 8), pl.ds(0, 32)], out_r, store_sem.at[1])
     store_r.start()
@@ -565,7 +554,7 @@
         V(1, 10, 16, 128), V(1, 10, 16, 128), V(2, 1, 10, 8, 128), V(10, 16, 128),
         V(3, narrow, 128), V(narrow, 3, narrow, 128), V(3, ring, group, narrow, 128),
         V(narrow, 128), V(narrow, narrow, 128), V(ring, group, narrow, 128), V(wide, narrow, 128),
-        V(wide, narrow, 128), V(wide, narrow, 128),
+        V(wide + 1, narrow, 128), V(wide, narrow, 128), V(wide, narrow, 128),
         V(wide + 4, narrow, 128), V(wide, narrow, 128), V(wide, narrow, 128), V(5, narrow, 128),
         pltpu.SemaphoreType.DMA((144,)), pltpu.SemaphoreType.DMA((144,)), pltpu.SemaphoreType.DMA((4,)),
         pltpu.SemaphoreType.DMA((2,)),
@@ -577,7 +566,7 @@
         in_specs=[anywhere] * 4,
         out_specs=(anywhere, anywhere),
         scratch_shapes=scratch,
-        compiler_params=pltpu.CompilerParams(collective_id=0, has_side_effects=True, vmem_limit_bytes=40 * 1024 * 1024),
+        compiler_params=pltpu.CompilerParams(collective_id=0, has_side_effects=True, vmem_limit_bytes=60 * 1024 * 1024),
     )(source, face_x, face_y, face_z)
 
 

time: 80.1 us -> 66.1 us (0.83)
  Pallas kernels: 73.7 us -> 62.2 us
  local copies, waits for them, and re-layouts: 5.2 us -> 2.42 us
    pallas_call x1, Pallas kernels: 73.7 us -> 62.2 us  [shards(): pl.pallas_call(functools.partial(body, sizes), out_shape=(shape, shape),...]
    unnamed x10 -> x4, local copies, waits for them, and re-layouts: 5.2 us -> 2.42 us
where the time goes in v2:
time: 66.1 us; the launch traced here: 65.3 us
  Pallas kernels  62.2 us (94%)
  local copies, waits for them, and re-layouts  2.42 us (4%)
    pallas_call x1, Pallas kernels, shards(): pl.pallas_call(functools.partial(body, sizes), out_shape=(shape, shape),...  62.2 us
    unnamed x4, local copies, waits for them, and re-layouts  2.42 us

profile of v2, /device:TPU:1, one launch (start us, length us, event | category | flops | bytes accessed | tf_op | source)
XLA Modules:
  0.0 65.3 jit_solution(15713526419513892010)
XLA Ops:
  0.6 62.2 %shard_map.59 = (f32[8,32,256]{2,1,0:T(8,128)}, f32[8,32,256]{2,1,0:T(8,128)}) custom-call(f32[8,32,256]{2,1,0:T(8,128)} %src.1, f32[8,32,256]{2,1,0:T(8,128)} %inx.1, f32[8,32,256]{2,1,0:T(8,128)} %iny.1, f32[8,32,256]{2,1,0:T(8,128)} %inz.1), custom_call_target="tpu_custom_call" | custom-call | tf_op jit(solution)/shard_map/pallas_call | solution.py:563
  62.9 0.0 copy-start
  62.9 1.7 %copy.8 = f32[8,32,256]{2,1,0:T(8,128)} copy(f32[8,32,256]{2,1,0:T(8,128)} %get-tuple-element.4) | data formatting | bytes 524288
  64.6 0.0 copy-done
  64.6 0.7 %copy.9 = f32[8,32,256]{2,1,0:T(8,128)} copy(f32[8,32,256]{2,1,0:T(8,128)S(1)} %copy-done) | data formatting | bytes 524288
Async XLA Ops:
  62.9 1.7 %copy-start = (f32[8,32,256]{2,1,0:T(8,128)S(1)}, f32[8,32,256]{2,1,0:T(8,128)}, u32[]{:S(2)}) copy-start(f32[8,32,256]{2,1,0:T(8,128)} %get-tuple-element.5) | copy-start | bytes 786436

commit v3 on v2

--- a/solution.py
+++ b/solution.py
@@ -114,15 +114,12 @@
         for copy in copies:
             copy.wait_recv()
 
-    def exchange(source, target, stage, own, rows, far):
-        near, later = [], []
-        for a in sorted(range(-far, far + 1), key=abs):
+    def exchange(source, target, stage, own, rows, steps):
+        copies = []
+        for a in steps:
             for b in (0, 1, -1):
                 if (a, b) == (0, 0):
                     continue
-                start = 4 - a * own
-                low, high = max(start, 0), min(start + own, 8 + own)
-                from_low = 4 + low - start
                 partner = (wide_at(-a), narrow_at(-b))
                 if b == 0:
                     piece = source.at[:, pl.ds(4, own), pl.ds(0, rows)]
@@ -130,9 +127,10 @@
                 else:
                     piece = source.at[:, pl.ds(4, own), pl.ds(rows - 8 if b == -1 else 0, 8)]
                     place = stage.at[0 if b == -1 else 1, :, pl.ds(4 + a * own, own)]
-                copy = send(piece, place, partner)
-                (near if abs(a) < 2 else later).append(copy)
-        return near, later
+                copies.append(send(piece, place, partner))
+        return copies
+
+    near, far = (0, 1, -1), (2, -2)
 
     tile_row = iota((8, 128), 0)
     row256 = iota((8, 256), 0)
@@ -205,10 +203,8 @@
                 target[number, 4 + c, 0:half] = got[c * half:(c + 1) * half]
 
     coarse_faces(IN, 3, F1, 4, 32, pairs0, odds0)
-    faces1, _ = exchange(F1, F1, F1S, 4, 16, 1)
+    faces1 = exchange(F1, F1, F1S, 4, 16, near)
     coarse_faces(F1, 4, F2, 2, 16, pairs1, odds1)
-    near, later = exchange(F2, F2, F2S, 2, 8, 2)
-    faces2 = near + later
 
     lane_block = iota((8, 128), 1) >> 5
     both_rows = (tile_row >> 1) == lane_block
@@ -267,14 +263,6 @@
     def down0(c):
         sweep(VD, VA, IN.at[3], IN, W0, 2 * c + 2, 2)
 
-    background = []
-    background.append(send(VD.at[pl.ds(8, 3), pl.ds(0, 32)], VB.at[pl.ds(0, 3)], (wide_at(1), j)))
-    background.append(send(VD.at[pl.ds(3, 3), pl.ds(0, 32)], VB.at[pl.ds(3, 3)], (wide_at(-1), j)))
-    for side, b, row in ((0, 1, 24), (1, -1, 0)):
-        background.append(send(VD.at[pl.ds(3, 8), pl.ds(row, 8)], VY.at[side, pl.ds(3, 8)], (i, narrow_at(b))))
-        background.append(send(VD.at[pl.ds(8, 3), pl.ds(row, 8)], VY.at[side, pl.ds(0, 3)], (wide_at(1), narrow_at(b))))
-        background.append(send(VD.at[pl.ds(3, 3), pl.ds(row, 8)], VY.at[side, pl.ds(11, 3)], (wide_at(-1), narrow_at(b))))
-
     @pl.loop(0, 4)
     def restrict0(c):
         both = remainder(IN.at[3], IN, VD, 2 * c + 3, 2)
@@ -284,7 +272,8 @@
     got = picked(got, pairs0)
     for c in range(4):
         B1[0, 4 + c, 0:16] = got[16 * c:16 * (c + 1)]
-    rhs1, _ = exchange(B1, B1, B1S, 4, 16, 1)
+    rhs1 = exchange(B1, B1, B1S, 4, 16, near)
+    faces2 = exchange(F2, F2, F2S, 2, 8, near + far)
 
     arrive(gather_f)
     sub = iota((narrow, 128), 0)
@@ -329,13 +318,12 @@
     for p in (-1, 2):
         sweep(Y1.at[0], X1, B1.at[0], F1, W1, p + 4, 3)
 
-    back1, _ = exchange(Y1, Y1R, Y1S, 4, 16, 1)
     rest = remainder(B1.at[0], F1, Y1.at[0], 4, 4)
     got = paired([rest[2 * c, :16] + rest[2 * c + 1, :16] for c in range(2)])
     got = picked(got, pairs1)
     for c in range(2):
         B2[0, 4 + c, 0:8] = got[8 * c:8 * (c + 1)]
-    rhs2, rhs2_far = exchange(B2, B2, B2S, 2, 8, 2)
+    rhs2 = exchange(B2, B2, B2S, 2, 8, near)
 
     arrive(gather_f)
     gather_f = [send(G3f.at[:, :, ri], G3f.at[:, :, ri], (zi * group + lax.rem(ri + d, group), j)) for d in range(1, group)]
@@ -352,7 +340,6 @@
     B2[0, 2:8, 8:16] = jnp.where(tile_row[None] < 4, B2S[1, 0, 2:8], B2S[0, 0, 2:8])
     X2[2:8] = W2[2:8] * B2[0, 2:8]
     sweep(Y2.at[0], X2, B2.at[0], F2, W2, 3, 4)
-    back2_near, back2_far = exchange(Y2, Y2R, Y2S, 2, 8, 2)
     rest = remainder(B2.at[0], F2, Y2.at[0], 4, 2)
     B3s[...] = to_row(rest[0, :8] + rest[1, :8], pairs2, both_rows)
     gather_b = [send(B3s, B3r.at[j], (i, narrow_at(d))) for d in range(1, narrow)]
@@ -380,6 +367,17 @@
 
     arrive(gather_b)
     gather_b = [send(G3b.at[:, ri], G3b.at[:, ri], (zi * group + lax.rem(ri + d, group), j)) for d in range(1, group)]
+
+    back2 = exchange(Y2, Y2R, Y2S, 2, 8, near + far) + exchange(B2, B2, B2S, 2, 8, far)
+    back1 = exchange(Y1, Y1R, Y1S, 4, 16, near)
+    background = []
+    background.append(send(VD.at[pl.ds(8, 3), pl.ds(0, 32)], VB.at[pl.ds(0, 3)], (wide_at(1), j)))
+    background.append(send(VD.at[pl.ds(3, 3), pl.ds(0, 32)], VB.at[pl.ds(3, 3)], (wide_at(-1), j)))
+    for side, b, row in ((0, 1, 24), (1, -1, 0)):
+        background.append(send(VD.at[pl.ds(3, 8), pl.ds(row, 8)], VY.at[side, pl.ds(3, 8)], (i, narrow_at(b))))
+        background.append(send(VD.at[pl.ds(8, 3), pl.ds(row, 8)], VY.at[side, pl.ds(0, 3)], (wide_at(1), narrow_at(b))))
+        background.append(send(VD.at[pl.ds(3, 3), pl.ds(row, 8)], VY.at[side, pl.ds(11, 3)], (wide_at(-1), narrow_at(b))))
+
     for p in (0, 1, wide + 2, wide + 3):
         PD[p] = jnp.zeros((narrow, 128), F32)
     for p in range(5):
@@ -456,7 +454,7 @@
         x = jnp.where(row16 < 8, middle, jnp.where(row16 < 12, above, below))
         spread.append(jnp.where(wanted, x, 0.0))
     spread = picked(jnp.concatenate(spread, axis=0), spread2)
-    arrive(rhs2_far + back2_near + back2_far)
+    arrive(back2)
     reach2 = inside(16, 128, 8, 4)
     for p in (0, 1, 8, 9):
         B2[0, p, 8:16] = merged(B2S, 0, p)

time: 66.1 us -> 67.8 us (1.026); the launches traced: 65.3 us -> 67.7 us
  Pallas kernels: 62.2 us -> 64.6 us
    pallas_call x1, Pallas kernels: 62.2 us -> 64.6 us  [shards(): pl.pallas_call(functools.partial(body, sizes), out_shape=(shape, shape),...]
where the time goes in v3:
time: 67.8 us; the launch traced here: 67.7 us
  Pallas kernels  64.6 us (95%)
  local copies, waits for them, and re-layouts  2.42 us (4%)
    pallas_call x1, Pallas kernels, shards(): pl.pallas_call(functools.partial(body, sizes), out_shape=(shape, shape),...  64.6 us
    unnamed x4, local copies, waits for them, and re-layouts  2.42 us

profile of v3, /device:TPU:1, one launch (start us, length us, event | category | flops | bytes accessed | tf_op | source)
XLA Modules:
  0.0 67.7 jit_solution(11210624119949148568)
XLA Ops:
  0.6 64.6 %shard_map.59 = (f32[8,32,256]{2,1,0:T(8,128)}, f32[8,32,256]{2,1,0:T(8,128)}) custom-call(f32[8,32,256]{2,1,0:T(8,128)} %src.1, f32[8,32,256]{2,1,0:T(8,128)} %inx.1, f32[8,32,256]{2,1,0:T(8,128)} %iny.1, f32[8,32,256]{2,1,0:T(8,128)} %inz.1), custom_call_target="tpu_custom_call" | custom-call | tf_op jit(solution)/shard_map/pallas_call | solution.py:561
  65.3 0.0 copy-start
  65.3 1.7 %copy.8 = f32[8,32,256]{2,1,0:T(8,128)} copy(f32[8,32,256]{2,1,0:T(8,128)} %get-tuple-element.4) | data formatting | bytes 524288
  67.0 0.0 copy-done
  67.0 0.7 %copy.9 = f32[8,32,256]{2,1,0:T(8,128)} copy(f32[8,32,256]{2,1,0:T(8,128)S(1)} %copy-done) | data formatting | bytes 524288
Async XLA Ops:
  65.3 1.7 %copy-start = (f32[8,32,256]{2,1,0:T(8,128)S(1)}, f32[8,32,256]{2,1,0:T(8,128)}, u32[]{:S(2)}) copy-start(f32[8,32,256]{2,1,0:T(8,128)} %get-tuple-element.5) | copy-start | bytes 786436

commit v4 on v3

--- a/solution.py
+++ b/solution.py
@@ -114,10 +114,10 @@
         for copy in copies:
             copy.wait_recv()
 
-    def exchange(source, target, stage, own, rows, steps):
+    def exchange(source, target, stage, own, rows, steps, sides=(0, 1, -1)):
         copies = []
         for a in steps:
-            for b in (0, 1, -1):
+            for b in sides:
                 if (a, b) == (0, 0):
                     continue
                 partner = (wide_at(-a), narrow_at(-b))
@@ -326,7 +326,7 @@
     rhs2 = exchange(B2, B2, B2S, 2, 8, near)
 
     arrive(gather_f)
-    gather_f = [send(G3f.at[:, :, ri], G3f.at[:, :, ri], (zi * group + lax.rem(ri + d, group), j)) for d in range(1, group)]
+    gather_f = [send(G3f.at[:, :, ri], G3f.at[:, :, ri], (zi * group + lax.rem(ri + d, group), j)) for d in range(2, group, 2)]
 
     arrive(faces2)
     finish_faces(F2, F2S, 10, 8)
@@ -344,10 +344,27 @@
     B3s[...] = to_row(rest[0, :8] + rest[1, :8], pairs2, both_rows)
     gather_b = [send(B3s, B3r.at[j], (i, narrow_at(d))) for d in range(1, narrow)]
     B3r[j] = B3s[...]
+
+    back2 = exchange(Y2, Y2R, Y2S, 2, 8, near + far, (0,)) + exchange(B2, B2, B2S, 2, 8, far, (0,))
+    back1 = exchange(Y1, Y1R, Y1S, 4, 16, near, (0,))
+    background = [
+        send(VD.at[pl.ds(8, 3), pl.ds(0, 32)], VB.at[pl.ds(0, 3)], (wide_at(1), j)),
+        send(VD.at[pl.ds(3, 3), pl.ds(0, 32)], VB.at[pl.ds(3, 3)], (wide_at(-1), j))]
     arrive(gather_b)
     G3b[zi, ri] = assembled([B3r[n] for n in range(narrow)])
     gather_b = [send(G3b.at[zi, ri], G3b.at[zi, ri], (lax.rem(zi + d, ring) * group + ri, j)) for d in range(1, ring)]
 
+    back2 += exchange(Y2, Y2R, Y2S, 2, 8, near + far, (1, -1)) + exchange(B2, B2, B2S, 2, 8, far, (1, -1))
+    back1 += exchange(Y1, Y1R, Y1S, 4, 16, near, (1, -1))
+    for side, b, row in ((0, 1, 24), (1, -1, 0)):
+        background.append(send(VD.at[pl.ds(3, 8), pl.ds(row, 8)], VY.at[side, pl.ds(3, 8)], (i, narrow_at(b))))
+        background.append(send(VD.at[pl.ds(8, 3), pl.ds(row, 8)], VY.at[side, pl.ds(0, 3)], (wide_at(1), narrow_at(b))))
+        background.append(send(VD.at[pl.ds(3, 3), pl.ds(row, 8)], VY.at[side, pl.ds(11, 3)], (wide_at(-1), narrow_at(b))))
+
+    arrive(gather_f)
+    core = lax.rem(i, 2)
+    sibling = (i + 1 - 2 * core, j)
+    gather_f = [send(G3f.at[:, :, 2 * c + core], G3f.at[:, :, 2 * c + core], sibling) for c in range(group // 2)]
     arrive(gather_f)
     block3 = iota((narrow, 128), 1) >> 5
     lane3 = iota((narrow, 128), 1) & 31
@@ -367,16 +384,6 @@
 
     arrive(gather_b)
     gather_b = [send(G3b.at[:, ri], G3b.at[:, ri], (zi * group + lax.rem(ri + d, group), j)) for d in range(1, group)]
-
-    back2 = exchange(Y2, Y2R, Y2S, 2, 8, near + far) + exchange(B2, B2, B2S, 2, 8, far)
-    back1 = exchange(Y1, Y1R, Y1S, 4, 16, near)
-    background = []
-    background.append(send(VD.at[pl.ds(8, 3), pl.ds(0, 32)], VB.at[pl.ds(0, 3)], (wide_at(1), j)))
-    background.append(send(VD.at[pl.ds(3, 3), pl.ds(0, 32)], VB.at[pl.ds(3, 3)], (wide_at(-1), j)))
-    for side, b, row in ((0, 1, 24), (1, -1, 0)):
-        background.append(send(VD.at[pl.ds(3, 8), pl.ds(row, 8)], VY.at[side, pl.ds(3, 8)], (i, narrow_at(b))))
-        background.append(send(VD.at[pl.ds(8, 3), pl.ds(row, 8)], VY.at[side, pl.ds(0, 3)], (wide_at(1), narrow_at(b))))
-        background.append(send(VD.at[pl.ds(3, 3), pl.ds(row, 8)], VY.at[side, pl.ds(11, 3)], (wide_at(-1), narrow_at(b))))
 
     for p in (0, 1, wide + 2, wide + 3):
         PD[p] = jnp.zeros((narrow, 128), F32)

time: 67.8 us -> 64.4 us (0.950)
  Pallas kernels: 64.6 us -> 61.1 us
    pallas_call x1, Pallas kernels: 64.6 us -> 61.1 us  [shards(): pl.pallas_call(functools.partial(body, sizes), out_shape=(shape, shape),...]
where the time goes in v4:
time: 64.4 us; the launch traced here: 64.2 us
  Pallas kernels  61.1 us (95%)
  local copies, waits for them, and re-layouts  2.42 us (4%)
  between operations  0.65 us (1%)
    pallas_call x1, Pallas kernels, shards(): pl.pallas_call(functools.partial(body, sizes), out_shape=(shape, shape),...  61.1 us
    unnamed x4, local copies, waits for them, and re-layouts  2.42 us

profile of v4, /device:TPU:1, one launch (start us, length us, event | category | flops | bytes accessed | tf_op | source)
XLA Modules:
  0.0 64.2 jit_solution(15412040071956444155)
XLA Ops:
  0.6 61.1 %shard_map.59 = (f32[8,32,256]{2,1,0:T(8,128)}, f32[8,32,256]{2,1,0:T(8,128)}) custom-call(f32[8,32,256]{2,1,0:T(8,128)} %src.1, f32[8,32,256]{2,1,0:T(8,128)} %inx.1, f32[8,32,256]{2,1,0:T(8,128)} %iny.1, f32[8,32,256]{2,1,0:T(8,128)} %inz.1), custom_call_target="tpu_custom_call" | custom-call | tf_op jit(solution)/shard_map/pallas_call | solution.py:568
  61.8 0.0 copy-start
  61.8 1.7 %copy.8 = f32[8,32,256]{2,1,0:T(8,128)} copy(f32[8,32,256]{2,1,0:T(8,128)} %get-tuple-element.4) | data formatting | bytes 524288
  63.5 0.0 copy-done
  63.5 0.7 %copy.9 = f32[8,32,256]{2,1,0:T(8,128)} copy(f32[8,32,256]{2,1,0:T(8,128)S(1)} %copy-done) | data formatting | bytes 524288
Async XLA Ops:
  61.8 1.7 %copy-start = (f32[8,32,256]{2,1,0:T(8,128)S(1)}, f32[8,32,256]{2,1,0:T(8,128)}, u32[]{:S(2)}) copy-start(f32[8,32,256]{2,1,0:T(8,128)} %get-tuple-element.5) | copy-start | bytes 786436

commit v5 on v4

--- a/solution.py
+++ b/solution.py
@@ -259,8 +259,7 @@
         W0[pl.ds(p + 3, 2)] = w
         VA[pl.ds(p + 3, 2)] = w * IN[3, pl.ds(p + 3, 2)]
 
-    @pl.loop(0, 5)
-    def down0(c):
+    for c in range(5):
         sweep(VD, VA, IN.at[3], IN, W0, 2 * c + 2, 2)
 
     @pl.loop(0, 4)
@@ -324,6 +323,7 @@
     for c in range(2):
         B2[0, 4 + c, 0:8] = got[8 * c:8 * (c + 1)]
     rhs2 = exchange(B2, B2, B2S, 2, 8, near)
+    early = len(sent)
 
     arrive(gather_f)
     gather_f = [send(G3f.at[:, :, ri], G3f.at[:, :, ri], (zi * group + lax.rem(ri + d, group), j)) for d in range(2, group, 2)]
@@ -389,6 +389,8 @@
         PD[p] = jnp.zeros((narrow, 128), F32)
     for p in range(5):
         XS[p] = jnp.zeros((narrow, 128), F32)
+    for copy in sent[:early]:
+        copy.wait_send()
     arrive(gather_b)
 
     def next_y3(cells):
@@ -411,9 +413,17 @@
         total = total + jnp.sum(r * r, axis=0)
     norm_first = summed(total)
 
-    def curvature(keep):
+    def curvature(beta):
+        def turn(a):
+            p = a * group
+            PD[p + 2:p + 2 + group] = RR[p:p + group] + beta * PD[p + 2:p + 2 + group]
+
+        if beta is not None:
+            turn(0)
         total = zero3
         for a in range(ring):
+            if beta is not None and a < ring - 1:
+                turn(a + 1)
             p = a * group
             here = PD[p + 2:p + 2 + group]
             high = XG[p + 1:p + 1 + group] * (here - PD[p + 3:p + 3 + group])
@@ -422,13 +432,13 @@
             along_z = ZG[p:p + group] * (here - pltpu.roll(here, 127, 2))
             q = (EG[p:p + group] * here + (high - low)) + (
                 (along_y - last_y3(along_y)) + (along_z - pltpu.roll(along_z, 1, 2)))
-            if keep:
-                QQ[p:p + group] = q
+            QQ[p:p + group] = q
             total = total + jnp.sum(here * q, axis=0)
         return summed(total)
 
-    def iteration(counter, norm_now):
-        alpha = norm_now / curvature(True)
+    def iteration(counter, carry):
+        norm_now, curved = carry
+        alpha = norm_now / curved
         for p in range(5):
             XS[p] = XS[p] + alpha * PD[i + p]
         total = zero3
@@ -438,14 +448,10 @@
             RR[planes] = r
             total = total + jnp.sum(r * r, axis=0)
         norm_next = summed(total)
-        beta = norm_next / norm_now
-        for a in range(ring):
-            p = a * group
-            PD[p + 2:p + 2 + group] = RR[p:p + group] + beta * PD[p + 2:p + 2 + group]
-        return norm_next
-
-    norm_now = lax.fori_loop(0, CGI - 1, iteration, norm_first)
-    alpha = norm_now / curvature(False)
+        return norm_next, curvature(norm_next / norm_now)
+
+    norm_now, curved = lax.fori_loop(0, CGI - 1, iteration, (norm_first, curvature(None)))
+    alpha = norm_now / curved
     for p in range(5):
         XS[p] = XS[p] + alpha * PD[i + p]
 
@@ -519,24 +525,21 @@
         VE[p] = corrected(p - 3, VB[p])
         VE[p + 11] = corrected(p + 8, VB[p + 3])
 
-    @pl.loop(0, 6)
-    def up0(c):
+    for c in range(6):
         sweep(VA, VE, IN.at[3], IN, W0, 2 * c + 1, 2)
 
-    @pl.loop(0, 5)
-    def up0_again(c):
+    for c in range(5):
         sweep(VF, VA, IN.at[3], IN, W0, 2 * c + 2, 2)
 
     store = pltpu.make_async_copy(VF.at[pl.ds(3, 8), pl.ds(0, 32)], out_p, store_sem.at[0])
     store.start()
 
-    @pl.loop(0, 4)
-    def rest0(c):
+    for c in range(4):
         VE[pl.ds(2 * c, 2)] = remainder(IN.at[3], IN, VF, 2 * c + 3, 2)
 
     store_r = pltpu.make_async_copy(VE.at[pl.ds(0, 8), pl.ds(0, 32)], out_r, store_sem.at[1])
     store_r.start()
-    for copy in sent:
+    for copy in sent[early:]:
         copy.wait_send()
     store.wait()
     store_r.wait()

time: 64.4 us -> 62.6 us (0.972)
  Pallas kernels: 61.1 us -> 59.3 us
    pallas_call x1, Pallas kernels: 61.1 us -> 59.3 us  [shards(): pl.pallas_call(functools.partial(body, sizes), out_shape=(shape, shape),...]
where the time goes in v5:
time: 62.6 us; the launch traced here: 62.4 us
  Pallas kernels  59.3 us (95%)
  local copies, waits for them, and re-layouts  2.42 us (4%)
  between operations  0.65 us (1%)
    pallas_call x1, Pallas kernels, shards(): pl.pallas_call(functools.partial(body, sizes), out_shape=(shape, shape),...  59.3 us
    unnamed x4, local copies, waits for them, and re-layouts  2.42 us

profile of v5, /device:TPU:1, one launch (start us, length us, event | category | flops | bytes accessed | tf_op | source)
XLA Modules:
  0.0 62.4 jit_solution(14653626167736126688)
XLA Ops:
  0.6 59.3 %shard_map.59 = (f32[8,32,256]{2,1,0:T(8,128)}, f32[8,32,256]{2,1,0:T(8,128)}) custom-call(f32[8,32,256]{2,1,0:T(8,128)} %src.1, f32[8,32,256]{2,1,0:T(8,128)} %inx.1, f32[8,32,256]{2,1,0:T(8,128)} %iny.1, f32[8,32,256]{2,1,0:T(8,128)} %inz.1), custom_call_target="tpu_custom_call" | custom-call | tf_op jit(solution)/shard_map/pallas_call | solution.py:571
  59.9 0.0 copy-start
  60.0 1.7 %copy.8 = f32[8,32,256]{2,1,0:T(8,128)} copy(f32[8,32,256]{2,1,0:T(8,128)} %get-tuple-element.4) | data formatting | bytes 524288
  61.7 0.0 copy-done
  61.7 0.7 %copy.9 = f32[8,32,256]{2,1,0:T(8,128)} copy(f32[8,32,256]{2,1,0:T(8,128)S(1)} %copy-done) | data formatting | bytes 524288
Async XLA Ops:
  59.9 1.7 %copy-start = (f32[8,32,256]{2,1,0:T(8,128)S(1)}, f32[8,32,256]{2,1,0:T(8,128)}, u32[]{:S(2)}) copy-start(f32[8,32,256]{2,1,0:T(8,128)} %get-tuple-element.5) | copy-start | bytes 786436
